TPU v7x, 256 devices: a whole 4x4x8 slice. The times are simulated.
256 devices in a mesh: pp: 4 (over y), node: 8 (over x, core), local: 8 (over z).
Axes of the slice: x: 4, y: 4, z: 8, core: 2. Of those that a mesh axis runs over, the one named last changes fastest.
Arguments:
- act_fwd: bfloat16 [4, 8192, 4096], P('pp', ('node', 'local')), may hold values from -6 to 6
- routes_fwd: int32 [4, 8192, 1], P('pp', ('node', 'local')), may hold values from 0 to 7; in each aligned block of 128 rows (0 to 127, 128 to 255, ..., all dimensions but the last counted through in order) at most 20 rows name the same one
- weight_fwd: float32 [4, 8192], P('pp', ('node', 'local')), may hold values from 0.25 to 1
- grad_bwd: bfloat16 [4, 8192, 4096], P('pp', ('node', 'local')), may hold values from -6 to 6
- routes_bwd: int32 [4, 8192, 1], P('pp', ('node', 'local')), may hold values from 0 to 7; in each aligned block of 128 rows (0 to 127, 128 to 255, ..., all dimensions but the last counted through in order) at most 20 rows name the same one
- weight_bwd: float32 [4, 8192], P('pp', ('node', 'local')), may hold values from 0.25 to 1
- saved_bwd: bfloat16 [4, 8192, 2048], P('pp', ('node', 'local')), may hold values from -8 to 8
- w_gate_up: bfloat16 [4, 8, 4096, 2048], P('pp', 'node', 'local'), may hold values from -0.09375 to 0.09375
- w_down: bfloat16 [4, 8, 1024, 4096], P('pp', 'node', None, 'local'), may hold values from -0.1875 to 0.1875
Outputs:
- next_input: bfloat16 [4, 8192, 4096], P('pp', ('node', 'local'))
- prev_grad: bfloat16 [4, 8192, 4096], P('pp', ('node', 'local'))
Inputs may be any that keep to these rules, and one draw needn't show every extreme that they name: `routes_fwd`: within each device's 128 tokens (aligned blocks of rows), no expert is named more than 20 times, a bound that some block reaches. `routes_bwd`: within each device's 128 tokens (aligned blocks of rows), no expert is named more than 20 times, a bound that some block reaches.
All inputs are finite; a program needn't handle non-finite values.
Results may differ from a plain program's by a relative error of at most 0.017.
Values may be sent and summed in bfloat16 or wider, within the bound.
A program may use at most 128 MiB of HBM per device.

v0:
```python
import jax
import jax.numpy as jnp
from jax import lax
from jax.sharding import PartitionSpec as P


def place_matrix(route, expert_count, capacity):
    rows = route.shape[0]
    same = route[:, None] == route[None, :]
    earlier = jnp.arange(rows, dtype=jnp.int32)[None, :] < jnp.arange(rows, dtype=jnp.int32)[:, None]
    slot_index = jnp.sum((same & earlier).astype(jnp.int32), axis=1)
    target = route * capacity + slot_index
    positions = jnp.arange(expert_count * capacity, dtype=jnp.int32)
    return (positions[:, None] == target[None, :]).astype(jnp.bfloat16)


def pack_rows(placer, values):
    return jnp.dot(placer, values, preferred_element_type=jnp.float32).astype(jnp.bfloat16)


def unpack_rows(placer, packed):
    return lax.dot_general(
        placer, packed, (((0,), (0,)), ((), ())), preferred_element_type=jnp.float32
    )


def swap(packed, nodes):
    blocks = packed.reshape(nodes, -1, packed.shape[1])
    return lax.all_to_all(blocks, "node", split_axis=0, concat_axis=0, tiled=True).reshape(packed.shape)


def body(
    act_fwd, routes_fwd, weight_fwd, grad_bwd, routes_bwd, weight_bwd, saved_bwd, w_gate_up, w_down
):
    nodes = lax.axis_size("node")
    capacity = 5 * act_fwd.shape[1] // (4 * nodes)
    w_gu = lax.all_gather(w_gate_up[0, 0], "local", axis=0, tiled=True)
    w_dn = lax.all_gather(w_down[0, 0], "local", axis=0, tiled=False)
    shards, hidden_units, column = w_dn.shape
    tokens = act_fwd[0]
    cotangent = grad_bwd[0]
    placer_a = place_matrix(routes_fwd[0, :, 0], nodes, capacity)
    placer_b = place_matrix(routes_bwd[0, :, 0], nodes, capacity)
    scaled = (weight_bwd[0][:, None] * cotangent.astype(jnp.float32)).astype(jnp.bfloat16)
    rows_a = swap(pack_rows(placer_a, tokens), nodes)
    rows_b = swap(pack_rows(placer_b, scaled), nodes)
    saved = swap(pack_rows(placer_b, saved_bwd[0]), nodes)
    grad_hidden = sum(
        lax.dot_general(
            rows_b[:, j * column : (j + 1) * column], w_dn[j], (((1,), (1,)), ((), ())),
            preferred_element_type=jnp.float32,
        )
        for j in range(shards)
    )
    gate_pre = saved[:, :hidden_units].astype(jnp.float32)
    up_pre = saved[:, hidden_units:].astype(jnp.float32)
    sigmoid_g = 1.0 / (1.0 + jnp.exp(-gate_pre))
    grad_gate = grad_hidden * up_pre * sigmoid_g * (1.0 + gate_pre * (1.0 - sigmoid_g))
    grad_up = grad_hidden * gate_pre * sigmoid_g
    grad_gu = jnp.concatenate([grad_gate, grad_up], axis=1).astype(jnp.bfloat16)
    done_b = lax.dot_general(
        grad_gu, w_gu, (((1,), (1,)), ((), ())), preferred_element_type=jnp.float32
    ).astype(jnp.bfloat16)
    preact = jnp.dot(rows_a, w_gu, preferred_element_type=jnp.float32)
    hidden = (jax.nn.silu(preact[:, :hidden_units]) * preact[:, hidden_units:]).astype(jnp.bfloat16)
    done_a = jnp.concatenate(
        [jnp.dot(hidden, w_dn[j], preferred_element_type=jnp.float32).astype(jnp.bfloat16) for j in range(shards)],
        axis=1,
    )
    moe_a = unpack_rows(placer_a, swap(done_a, nodes))
    moe_b = unpack_rows(placer_b, swap(done_b, nodes))
    result_a = (tokens.astype(jnp.float32) + weight_fwd[0][:, None] * moe_a).astype(jnp.bfloat16)
    result_b = (cotangent.astype(jnp.float32) + moe_b).astype(jnp.bfloat16)
    length = lax.axis_size("pp")
    next_input = lax.ppermute(result_a[None], "pp", [(i, (i + 1) % length) for i in range(length)])
    prev_grad = lax.ppermute(result_b[None], "pp", [(i, (i - 1) % length) for i in range(length)])
    return (next_input, prev_grad)


def solution(mesh):
    in_specs = (
        P("pp", ("node", "local"), None),
        P("pp", ("node", "local"), None),
        P("pp", ("node", "local")),
        P("pp", ("node", "local"), None),
        P("pp", ("node", "local"), None),
        P("pp", ("node", "local")),
        P("pp", ("node", "local"), None),
        P("pp", "node", "local", None),
        P("pp", "node", None, "local"),
    )
    out_specs = (P("pp", ("node", "local"), None), P("pp", ("node", "local"), None))
    return jax.shard_map(body, mesh=mesh, in_specs=in_specs, out_specs=out_specs, check_vma=False)
```

profile of v0, /device:TPU:1, one launch (start us, length us, event | category | flops | bytes accessed | tf_op | source)
XLA Modules:
  0.0 383.1 jit_solution(13642669705079317526)
XLA Ops:
  7.2 0.0 copy-start
  7.2 0.0 all-gather.7.cloned.1.call-start
  7.2 0.7 all-gather.7.cloned.1.call-update
  7.9 0.0 all-gather.5.cloned.1.call-start
  8.0 0.7 all-gather.5.cloned.1.call-update
  8.7 0.2 convert_reduce_fusion
  8.9 0.3 convolution_convert_fusion.2
  9.2 0.0 copy-start.4
  9.2 0.0 copy-start.7
  9.2 1.0 reshape.64
  10.2 7.3 %all-to-all-start.3 = ((bf16[8,20,2048]{2,1,0:T(8,128)(2,1)}), bf16[8,20,2048]{2,1,0:T(8,128)(2,1)}, u32[]{:S(2)}, u32[]{:S(2)}) async-start(bf16[8,20,2048]{2,1,0:T(8,128)(2,1)} %reshape.64), calls=%async_computation.3 | async-start | bytes 1572864 | tf_op jit(solution)/shard_map/all_to_all | solution.py:29
  17.6 0.0 copy-done.7
  17.6 0.6 convolution_convert_fusion
  18.2 1.3 reshape.62
  19.5 10.5 %all-to-all-done.3 = bf16[8,20,2048]{2,1,0:T(8,128)(2,1)} async-done(((bf16[8,20,2048]{2,1,0:T(8,128)(2,1)}), bf16[8,20,2048]{2,1,0:T(8,128)(2,1)}, u32[]{:S(2)}, u32[]{:S(2)}) %all-to-all-start.3) | async-done | bytes 655392 | tf_op jit(solution)/shard_map/all_to_all | solution.py:29
  30.0 4.4 %all-to-all-start.2 = ((bf16[8,20,4096]{2,1,0:T(8,128)(2,1)}), bf16[8,20,4096]{2,1,0:T(8,128)(2,1)S(1)}, u32[]{:S(2)}, u32[]{:S(2)}) async-start(bf16[8,20,4096]{2,1,0:T(8,128)(2,1)} %reshape.62), calls=%async_computation.2 | async-start | bytes 3145728 | tf_op jit(solution)/shard_map/all_to_all | solution.py:29
  34.4 0.2 convert_reduce_fusion.1
  34.5 1.7 convolution_convert_fusion.1
  36.3 1.4 reshape.58
  37.6 17.4 %all-to-all-done.2 = bf16[8,20,4096]{2,1,0:T(8,128)(2,1)S(1)} async-done(((bf16[8,20,4096]{2,1,0:T(8,128)(2,1)}), bf16[8,20,4096]{2,1,0:T(8,128)(2,1)S(1)}, u32[]{:S(2)}, u32[]{:S(2)}) %all-to-all-start.2) | async-done | bytes 1310752 | tf_op jit(solution)/shard_map/all_to_all | solution.py:29
  55.1 5.0 %all-to-all-start = ((bf16[8,20,4096]{2,1,0:T(8,128)(2,1)}), bf16[8,20,4096]{2,1,0:T(8,128)(2,1)}, u32[]{:S(2)}, u32[]{:S(2)}) async-start(bf16[8,20,4096]{2,1,0:T(8,128)(2,1)} %reshape.58), calls=%async_computation | async-start | bytes 3145728 | tf_op jit(solution)/shard_map/all_to_all | solution.py:29
  60.1 2.0 reshape.65
  62.1 0.3 reshape.63
  62.4 18.5 %all-to-all-done = bf16[8,20,4096]{2,1,0:T(8,128)(2,1)} async-done(((bf16[8,20,4096]{2,1,0:T(8,128)(2,1)}), bf16[8,20,4096]{2,1,0:T(8,128)(2,1)}, u32[]{:S(2)}, u32[]{:S(2)}) %all-to-all-start) | async-done | bytes 1310752 | tf_op jit(solution)/shard_map/all_to_all | solution.py:29
  81.0 1.5 reshape.59
  82.5 25.3 %all-gather.7.cloned.1.call-done = bf16[8,1,1024,512]{3,2,1,0:T(8,128)(2,1)} async-done(((bf16[1,1,1024,512]{3,2,1,0:T(8,128)(2,1)}), bf16[8,1,1024,512]{3,2,1,0:T(8,128)(2,1)}) %all-gather.7.cloned.1.call-update) | async-done | bytes 8388624 | tf_op jit(solution)/shard_map/all_gather | solution.py:38
  107.8 1.9 fusion.25
  109.6 2.1 convolution_add_fusion.7
  111.8 1.7 convolution_add_fusion.6
  113.5 1.7 convolution_add_fusion.5
  115.2 0.5 convolution_add_fusion.4
  115.7 0.5 convolution_add_fusion.3
  116.2 0.0 copy-start.5
  116.2 0.5 convolution_add_fusion.2
  116.7 0.6 copy-done.5
  117.3 1.3 fusion.31
  118.7 162.3 %all-gather.5.cloned.1.call-done = bf16[1,1,4096,2048]{3,2,1,0:T(8,128)(2,1)} async-done(((bf16[1,1,512,2048]{3,2,1,0:T(8,128)(2,1)}), bf16[1,1,4096,2048]{3,2,1,0:T(8,128)(2,1)}) %all-gather.5.cloned.1.call-update) | async-done | bytes 16777232 | tf_op jit(solution)/shard_map/all_gather | solution.py:37
  281.0 11.6 %fusion.5 = bf16[160,4096]{1,0:T(8,128)(2,1)S(1)} fusion(bf16[1,1,4096,2048]{3,2,1,0:T(8,128)(2,1)} %all-gather.5.cloned.1.call-done, bf16[160,1024]{1,0:T(8,128)(2,1)} %get-tuple-element.3, bf16[160,1024]{1,0:T(8,128)(2,1)S(1)} %get-tuple-element.2), kind=kOutput, calls=%fused_computation.7 | convolution fusion | flops 2686320640 | bytes 18743296 | tf_op jit(solution)/shard_map/dot_general | solution.py:61
  292.5 1.4 reshape.66
  293.9 4.9 %all-to-all-start.4 = ((bf16[8,20,4096]{2,1,0:T(8,128)(2,1)}), bf16[8,20,4096]{2,1,0:T(8,128)(2,1)S(1)}, u32[]{:S(2)}, u32[]{:S(2)}) async-start(bf16[8,20,4096]{2,1,0:T(8,128)(2,1)} %reshape.66), calls=%async_computation.4 | async-start | bytes 3145728 | tf_op jit(solution)/shard_map/all_to_all | solution.py:29
  298.8 7.3 %fusion.2 = f32[160,2048]{1,0:T(8,128)S(1)} fusion(bf16[160,4096]{1,0:T(8,128)(2,1)S(1)} %reshape.59, bf16[1,1,4096,2048]{3,2,1,0:T(8,128)(2,1)} %all-gather.5.cloned.1.call-done), kind=kOutput, calls=%fused_computation.2 | convolution fusion | flops 2684354560 | bytes 19398656 | tf_op jit(solution)/shard_map/dot_general | solution.py:64
  306.1 0.2 fusion.34
  306.3 1.6 fusion.20
  307.9 1.6 fusion.19
  309.5 1.6 fusion.18
  311.0 1.6 fusion.17
  312.6 1.6 fusion.16
  314.2 1.6 fusion.15
  315.7 1.6 fusion.14
  317.3 1.6 fusion.13
  318.9 1.3 reshape.60
  320.2 0.0 all-to-all-done.4
  320.2 4.8 %all-to-all-start.1 = ((bf16[8,20,4096]{2,1,0:T(8,128)(2,1)}), bf16[8,20,4096]{2,1,0:T(8,128)(2,1)}, u32[]{:S(2)}, u32[]{:S(2)}) async-start(bf16[8,20,4096]{2,1,0:T(8,128)(2,1)} %reshape.60), calls=%async_computation.1 | async-start | bytes 3145728 | tf_op jit(solution)/shard_map/all_to_all | solution.py:29
  325.0 0.3 reshape.67
  325.3 2.7 fusion.10
  328.0 2.5 collective-permute-start.1
  330.5 15.4 %all-to-all-done.1 = bf16[8,20,4096]{2,1,0:T(8,128)(2,1)} async-done(((bf16[8,20,4096]{2,1,0:T(8,128)(2,1)}), bf16[8,20,4096]{2,1,0:T(8,128)(2,1)}, u32[]{:S(2)}, u32[]{:S(2)}) %all-to-all-start.1) | async-done | bytes 1310752 | tf_op jit(solution)/shard_map/all_to_all | solution.py:29
  345.8 1.5 reshape.61
  347.4 0.5 fusion.11
  347.9 1.3 collective-permute-start
  349.2 4.2 %collective-permute-done.1 = bf16[1,128,4096]{2,1,0:T(8,128)(2,1)} collective-permute-done((bf16[1,128,4096]{2,1,0:T(8,128)(2,1)}, bf16[1,128,4096]{2,1,0:T(8,128)(2,1)}, u32[]{:S(2)}, u32[]{:S(2)}) %collective-permute-start.1) | collective-permute-done | bytes 1048608 | tf_op jit(solution)/shard_map/ppermute | solution.py:76
  353.4 19.6 %collective-permute-done = bf16[1,128,4096]{2,1,0:T(8,128)(2,1)S(1)} collective-permute-done((bf16[1,128,4096]{2,1,0:T(8,128)(2,1)S(1)}, bf16[1,128,4096]{2,1,0:T(8,128)(2,1)S(1)}, u32[]{:S(2)}, u32[]{:S(2)}) %collective-permute-start) | collective-permute-done | bytes 1048608 | tf_op jit(solution)/shard_map/ppermute | solution.py:75
  373.0 1.0 copy.20
  374.0 2.3 copy.21
  (16 shorter events, 0.0 us)
Async XLA Ops:
  7.2 1.7 copy-start
  7.2 100.6 %all-gather.7.cloned.1.call-start = ((), (), s32[]{:S(2)}) async-start(), calls=%async_computation.6 | async-start | bytes 9437184 | tf_op jit(solution)/shard_map/all_gather | solution.py:38
  7.9 0.8 copy-start.8
  7.9 273.0 %all-gather.5.cloned.1.call-start = ((), (), s32[]{:S(2)}) async-start(), calls=%async_computation.5 | async-start | bytes 18874368 | tf_op jit(solution)/shard_map/all_gather | solution.py:37
  9.2 8.4 %copy-start.4 = (bf16[1,128,4096]{2,1,0:T(8,128)(2,1)S(1)}, bf16[1,128,4096]{2,1,0:T(8,128)(2,1)}, u32[]{:S(2)}) copy-start(bf16[1,128,4096]{2,1,0:T(8,128)(2,1)} %param.12) | copy-start | bytes 3145732
  9.2 8.4 %copy-start.7 = (f32[1,128]{1,0:T(1,128)S(1)}, f32[1,128]{1,0:T(1,128)}, u32[]{:S(2)}) copy-start(f32[1,128]{1,0:T(1,128)} %param.14) | copy-start | bytes 1540
  10.2 19.7 %all-to-all-start.3 = ((bf16[8,20,2048]{2,1,0:T(8,128)(2,1)}), bf16[8,20,2048]{2,1,0:T(8,128)(2,1)}, u32[]{:S(2)}, u32[]{:S(2)}) async-start(bf16[8,20,2048]{2,1,0:T(8,128)(2,1)} %reshape.64), calls=%async_computation.3 | async-start | bytes 1572864 | tf_op jit(solution)/shard_map/all_to_all | solution.py:29
  19.5 14.9 %copy-start.9 = (s32[1,128,1]{1,2,0:T(1,128)S(1)}, s32[1,128,1]{1,2,0:T(1,128)}, u32[]{:S(2)}) copy-start(s32[1,128,1]{1,2,0:T(1,128)} %param.10) | copy-start | bytes 1540
  30.0 25.1 %all-to-all-start.2 = ((bf16[8,20,4096]{2,1,0:T(8,128)(2,1)}), bf16[8,20,4096]{2,1,0:T(8,128)(2,1)S(1)}, u32[]{:S(2)}, u32[]{:S(2)}) async-start(bf16[8,20,4096]{2,1,0:T(8,128)(2,1)} %reshape.62), calls=%async_computation.2 | async-start | bytes 3145728 | tf_op jit(solution)/shard_map/all_to_all | solution.py:29
  55.1 25.9 %all-to-all-start = ((bf16[8,20,4096]{2,1,0:T(8,128)(2,1)}), bf16[8,20,4096]{2,1,0:T(8,128)(2,1)}, u32[]{:S(2)}, u32[]{:S(2)}) async-start(bf16[8,20,4096]{2,1,0:T(8,128)(2,1)} %reshape.58), calls=%async_computation | async-start | bytes 3145728 | tf_op jit(solution)/shard_map/all_to_all | solution.py:29
  107.8 7.4 %copy-start.2 = (bf16[8,1,1024,512]{3,2,1,0:T(8,128)(2,1)S(1)}, bf16[8,1,1024,512]{3,2,1,0:T(8,128)(2,1)}, u32[]{:S(2)}) copy-start(bf16[8,1,1024,512]{3,2,1,0:T(8,128)(2,1)} %all-gather.7.cloned.1.call-done) | copy-start | bytes 25165828
  116.2 1.1 copy-start.5
  293.9 26.3 %all-to-all-start.4 = ((bf16[8,20,4096]{2,1,0:T(8,128)(2,1)}), bf16[8,20,4096]{2,1,0:T(8,128)(2,1)S(1)}, u32[]{:S(2)}, u32[]{:S(2)}) async-start(bf16[8,20,4096]{2,1,0:T(8,128)(2,1)} %reshape.66), calls=%async_computation.4 | async-start | bytes 3145728 | tf_op jit(solution)/shard_map/all_to_all | solution.py:29
  320.2 25.6 %all-to-all-start.1 = ((bf16[8,20,4096]{2,1,0:T(8,128)(2,1)}), bf16[8,20,4096]{2,1,0:T(8,128)(2,1)}, u32[]{:S(2)}, u32[]{:S(2)}) async-start(bf16[8,20,4096]{2,1,0:T(8,128)(2,1)} %reshape.60), calls=%async_computation.1 | async-start | bytes 3145728 | tf_op jit(solution)/shard_map/all_to_all | solution.py:29
  328.0 19.4 %copy-start.3 = (bf16[1,128,4096]{2,1,0:T(8,128)(2,1)S(1)}, bf16[1,128,4096]{2,1,0:T(8,128)(2,1)}, u32[]{:S(2)}) copy-start(bf16[1,128,4096]{2,1,0:T(8,128)(2,1)} %param.9) | copy-start | bytes 3145732
  328.0 19.4 %copy-start.6 = (f32[1,128]{1,0:T(1,128)S(1)}, f32[1,128]{1,0:T(1,128)}, u32[]{:S(2)}) copy-start(f32[1,128]{1,0:T(1,128)} %param.11) | copy-start | bytes 1540
  328.0 25.4 %collective-permute-start.1 = (bf16[1,128,4096]{2,1,0:T(8,128)(2,1)}, bf16[1,128,4096]{2,1,0:T(8,128)(2,1)}, u32[]{:S(2)}, u32[]{:S(2)}) collective-permute-start(bf16[1,128,4096]{2,1,0:T(8,128)(2,1)} %fusion.10), channel_id=1, source_target_pairs={{0,192},{64,0},{128,64},{192,128},{1,193},{65,1},{129,65},{193,129... | collective-permute-start | bytes 3145736 | tf_op jit(solution)/shard_map/ppermute | solution.py:76
  347.9 25.1 %collective-permute-start = (bf16[1,128,4096]{2,1,0:T(8,128)(2,1)S(1)}, bf16[1,128,4096]{2,1,0:T(8,128)(2,1)S(1)}, u32[]{:S(2)}, u32[]{:S(2)}) collective-permute-start(bf16[1,128,4096]{2,1,0:T(8,128)(2,1)S(1)} %fusion.11), channel_id=1, source_target_pairs={{0,64},{64,128},{128,192},{192,0},{1,65},{65,129},{129,193},{193,1... | collective-permute-start | bytes 3145736 | tf_op jit(solution)/shard_map/ppermute | solution.py:75
  373.0 3.3 copy-start.1
Sparse Core Ops, SparseCore 0:
  9.8 97.9 all-gather.6
  109.6 171.3 all-gather.4
where the time goes:
time: 384 us; the launch traced here: 383 us
  waiting for transfers between devices  275 us (72%)
  matrix products  47.5 us (12%)
  starting transfers between devices  30.3 us (8%)
  local copies, waits for them, and re-layouts  15.9 us (4%)
  between operations  14.3 us (4%)
    all_gather x1, waiting for transfers between devices, body(): w_gu = lax.all_gather(w_gate_up[0, 0], 'local', axis=0, tiled=True)  162 us
    all_to_all x5, waiting for transfers between devices, swap(): lax.all_to_all(blocks, 'node', split_axis=0, concat_axis=0, tiled=True)  61.8 us
    all_to_all x5, starting transfers between devices, swap(): lax.all_to_all(blocks, 'node', split_axis=0, concat_axis=0, tiled=True)  26.4 us
    all_gather x1, waiting for transfers between devices, body(): w_dn = lax.all_gather(w_down[0, 0], 'local', axis=0, tiled=False)  25.3 us
    ppermute x1, waiting for transfers between devices, body(): lax.ppermute(result_a[None], 'pp', [(i, (i + 1) % length) for i in range(...  19.6 us
    dot_general x8, matrix products, body(): jnp.dot(hidden, w_dn[j], preferred_element_type=jnp.float32)  12.5 us
    dot_general x1, matrix products, body(): lax.dot_general(grad_gu, w_gu, (((1,), (1,)), ((), ())), preferred_elemen...  11.6 us
    dot_general x8, matrix products, body(): lax.dot_general(rows_b[:, j * column:(j + 1) * column], w_dn[j], (((1,),...  10.3 us
  transfers between devices with their start and end apart: 9, of which 8 were waited for; matrix products, arithmetic and copies ran while one was open for 12% of the time, Pallas kernels for 0%

commit v1 on v0

v1 whole, which is shorter than its diff:
```python
import functools

import jax
import jax.numpy as jnp
from jax import lax
from jax.experimental import pallas as pl
from jax.experimental.pallas import tpu as pltpu
from jax.sharding import PartitionSpec as P

MESH = pl.DeviceIdType.MESH
ROWS = 32
NT = (((1,), (1,)), ((), ()))


def kernel(
    act, route_a, weight_a, grad, route_b, weight_b, saved, w_gu, w_dn,
    out_a, out_b,
    act_v, grad_v, saved_v, gu_v, dn_v, xs_a, xr_a, xs_b, xr_b, ss, sr, back_a, back_b, res_a, res_b,
    pre, dh, dgu, hid, pick_a, pick_b, scale_a,
    load_sem, disp_send, disp_recv, dn_send, dn_recv, gu_send, gu_recv,
    ret_a_send, ret_a_recv, ret_b_send, ret_b_recv, relay_send, relay_recv,
):
    n_pp, n_node, n_local = lax.axis_size("pp"), lax.axis_size("node"), lax.axis_size("local")
    pp, node, me = lax.axis_index("pp"), lax.axis_index("node"), lax.axis_index("local")
    tokens, features = act.shape
    hidden = w_dn.shape[0]
    column = w_dn.shape[1]
    total = n_node * ROWS
    half = n_local // 2

    def wrap(index, size):
        return lax.rem(index + size, size)

    right, left = wrap(me + 1, n_local), wrap(me - 1, n_local)
    ahead, behind = wrap(pp + 1, n_pp), wrap(pp - 1, n_pp)
    peers = [wrap(node + k, n_node) for k in range(1, n_node)]

    loads = [
        pltpu.make_async_copy(grad, grad_v, load_sem.at[0]),
        pltpu.make_async_copy(saved, saved_v, load_sem.at[1]),
        pltpu.make_async_copy(act, act_v, load_sem.at[2]),
        pltpu.make_async_copy(w_dn, dn_v.at[me], load_sem.at[3]),
        pltpu.make_async_copy(w_gu, gu_v.at[me], load_sem.at[4]),
    ]

    barrier = pltpu.get_barrier_semaphore()
    for peer in peers:
        pl.semaphore_signal(barrier, inc=1, device_id={"node": peer}, device_id_type=MESH)
    for neighbour in (left, right):
        pl.semaphore_signal(barrier, inc=1, device_id={"local": neighbour}, device_id_type=MESH)
    for neighbour in (behind, ahead):
        pl.semaphore_signal(barrier, inc=1, device_id={"pp": neighbour}, device_id_type=MESH)
    for load in loads:
        load.start()
    pl.semaphore_wait(barrier, n_node - 1 + 4)

    def hop(buffer, send, recv, way, far, chunk, source=None):
        owner = wrap(me - far, n_local) if way == 0 else wrap(me + far, n_local)
        size = buffer.shape[1] // 2
        here = buffer.at[owner, pl.ds(chunk * size, size), :]
        slot = (way * half + far) * 2 + chunk
        return pltpu.make_async_remote_copy(
            src_ref=here if source is None else source.at[pl.ds(chunk * size, size), :],
            dst_ref=here,
            send_sem=send.at[slot],
            recv_sem=recv.at[slot],
            device_id={"local": right if way == 0 else left},
            device_id_type=MESH,
        )

    def landed(buffer, send, recv, way, far, chunk):
        owner = wrap(me - far, n_local) if way == 0 else wrap(me + far, n_local)
        size = buffer.shape[1] // 2
        here = buffer.at[owner, pl.ds(chunk * size, size), :]
        slot = (way * half + far - 1) * 2 + chunk
        return pltpu.make_async_remote_copy(
            src_ref=here, dst_ref=here, send_sem=send.at[slot], recv_sem=recv.at[slot],
            device_id={"local": right if way == 0 else left}, device_id_type=MESH,
        )

    dn = (dn_v, dn_send, dn_recv)
    gu = (gu_v, gu_send, gu_recv)

    def ring_start(ring, source):
        for chunk in range(2):
            for way in range(2):
                hop(*ring, way, 0, chunk, source).start()

    def ring_step(ring, far):
        for chunk in range(2):
            for way in range(2):
                landed(*ring, way, far, chunk).wait_recv()
                if chunk == way:
                    hop(*ring, way, far, chunk).start()
                else:
                    @pl.when(far < half - 1)
                    def _():
                        hop(*ring, way, far, chunk).start()

    def ring_last(ring):
        for way in range(2):
            landed(*ring, way, half, way).wait_recv()

    def ring_drain(ring):
        for far in range(half):
            for chunk in range(2):
                for way in range(2):
                    if far < half - 1 or chunk == way:
                        hop(*ring, way, far, chunk).wait_send()

    ring_start(dn, w_dn)

    def places(route_ref):
        route = jnp.broadcast_to(route_ref[...].astype(jnp.float32), (tokens, tokens))
        turned = jnp.transpose(route)
        first = lax.broadcasted_iota(jnp.int32, (tokens, tokens), 0)
        second = lax.broadcasted_iota(jnp.int32, (tokens, tokens), 1)
        same = route == turned
        slot_row = jnp.sum(jnp.where(same & (first < second), 1.0, 0.0), axis=0, keepdims=True)
        slot_col = jnp.sum(jnp.where(same & (second < first), 1.0, 0.0), axis=1, keepdims=True)
        row = route[0:1, :] * float(ROWS) + slot_row
        col = turned[:, 0:1] * float(ROWS) + slot_col
        put = lax.broadcasted_iota(jnp.int32, (total, tokens), 0).astype(jnp.float32) == row
        pick = lax.broadcasted_iota(jnp.int32, (tokens, total), 1).astype(jnp.float32) == col
        one, zero = jnp.float32(1), jnp.float32(0)
        return (
            jnp.where(put, one, zero).astype(jnp.bfloat16),
            jnp.where(pick, one, zero).astype(jnp.bfloat16),
        )

    def spread(weight_ref):
        turned = jnp.transpose(jnp.broadcast_to(weight_ref[...], (tokens, tokens)))
        return jnp.concatenate([turned] * (column // tokens), axis=1)

    def cols(block, width=None):
        width = column if width is None else width
        return pl.ds(pl.multiple_of(block * width, width), width)

    def at_node(index):
        return pl.ds(pl.multiple_of(index * ROWS, ROWS), ROWS)

    def dispatch(source, target, slot):
        for peer in peers:
            pltpu.make_async_remote_copy(
                src_ref=source.at[at_node(peer), :],
                dst_ref=target.at[at_node(node), :],
                send_sem=disp_send.at[slot],
                recv_sem=disp_recv.at[slot],
                device_id={"node": peer},
                device_id_type=MESH,
            ).start()
        target[at_node(node), :] = source[at_node(node), :]

    others = total - ROWS

    def all_of(buffer, sem, columns=slice(None)):
        part = buffer.at[pl.ds(0, others), columns]
        return pltpu.make_async_copy(part, part, sem)

    put_b, pick = places(route_b)
    pick_b[...] = pick
    scale_b = spread(weight_b)
    loads[0].wait()

    for block in range(features // column):
        at = slice(block * column, (block + 1) * column)
        scaled = (scale_b * grad_v[:, at].astype(jnp.float32)).astype(jnp.bfloat16)
        xs_b[:, at] = jnp.dot(put_b, scaled, preferred_element_type=jnp.float32).astype(jnp.bfloat16)
    dispatch(xs_b, xr_b, 0)
    loads[1].wait()
    for block in range(2 * hidden // column):
        at = slice(block * column, (block + 1) * column)
        ss[:, at] = jnp.dot(put_b, saved_v[:, at], preferred_element_type=jnp.float32).astype(jnp.bfloat16)
    dispatch(ss, sr, 1)
    put_a, pick = places(route_a)
    pick_a[...] = pick
    scale_a[...] = spread(weight_a)
    loads[2].wait()
    for block in range(features // column):
        at = slice(block * column, (block + 1) * column)
        xs_a[:, at] = jnp.dot(put_a, act_v[:, at], preferred_element_type=jnp.float32).astype(jnp.bfloat16)
    dispatch(xs_a, xr_a, 2)

    ring_step(dn, 1)
    ring_step(dn, 2)
    ring_start(gu, w_gu)
    ring_step(dn, 3)
    ring_last(dn)
    loads[3].wait()
    all_of(xr_b, disp_recv.at[0]).wait()

    dh[...] = jnp.zeros_like(dh)

    @pl.loop(0, n_local)
    def _(block):
        dh[...] += lax.dot_general(
            xr_b[:, cols(block)], dn_v[block], NT, preferred_element_type=jnp.float32
        )

    all_of(sr, disp_recv.at[1]).wait()

    part = 256

    @pl.loop(0, hidden // part)
    def _(index):
        at = cols(index, part)
        up_at = pl.ds(pl.multiple_of(hidden + index * part, part), part)
        gate = sr[:, at].astype(jnp.float32)
        up = sr[:, up_at].astype(jnp.float32)
        grad_h = dh[:, at]
        sigmoid = 1.0 / (1.0 + jnp.exp(-gate))
        dgu[:, at] = (grad_h * up * sigmoid * (1.0 + gate * (1.0 - sigmoid))).astype(jnp.bfloat16)
        dgu[:, up_at] = (grad_h * gate * sigmoid).astype(jnp.bfloat16)

    for slot, buffer in ((0, xs_b), (1, ss), (2, xs_a)):
        all_of(buffer, disp_send.at[slot]).wait()
    all_of(xr_a, disp_recv.at[2]).wait()
    pre[...] = jnp.zeros_like(pre)

    def forward(block):
        x = xr_a[:, cols(block)]

        @pl.loop(0, 2 * hidden // 512)
        def _(index):
            at = cols(index, 512)
            pre[:, at] += jnp.dot(x, gu_v[block, :, at], preferred_element_type=jnp.float32)

    def give_back(source, target, send, recv, block):
        for peer in peers:
            pltpu.make_async_remote_copy(
                src_ref=source.at[at_node(peer), cols(block)],
                dst_ref=target.at[at_node(node), cols(block)],
                send_sem=send.at[block],
                recv_sem=recv.at[block],
                device_id={"node": peer},
                device_id_type=MESH,
            ).start()
        target[at_node(node), cols(block)] = source[at_node(node), cols(block)]

    def backward(block):
        xs_b[:, cols(block)] = lax.dot_general(
            dgu[...], gu_v[block], NT, preferred_element_type=jnp.float32
        ).astype(jnp.bfloat16)
        give_back(xs_b, back_b, ret_b_send, ret_b_recv, block)

    def relay(source, target, slot, to, block):
        return pltpu.make_async_remote_copy(
            src_ref=source.at[:, cols(block)],
            dst_ref=target.at[:, cols(block)],
            send_sem=relay_send.at[slot],
            recv_sem=relay_recv.at[slot],
            device_id={"pp": to},
            device_id_type=MESH,
        )

    def finish_b(block):
        all_of(back_b, ret_b_recv.at[block], cols(block)).wait()
        moe = jnp.dot(pick_b[...], back_b[:, cols(block)], preferred_element_type=jnp.float32)
        res_b[:, cols(block)] = (grad_v[:, cols(block)].astype(jnp.float32) + moe).astype(jnp.bfloat16)
        relay(res_b, out_b, 1, behind, block).start()

    def finish_a(block):
        all_of(back_a, ret_a_recv.at[block], cols(block)).wait()
        moe = jnp.dot(pick_a[...], back_a[:, cols(block)], preferred_element_type=jnp.float32)
        res_a[:, cols(block)] = (
            act_v[:, cols(block)].astype(jnp.float32) + scale_a[...] * moe
        ).astype(jnp.bfloat16)
        relay(res_a, out_a, 0, ahead, block).start()

    def block_at(turn):
        far = (turn + 1) // 2
        return wrap(me + jnp.where(turn % 2 == 1, -far, far), n_local)

    loads[4].wait()

    @pl.loop(0, half)
    def _(far):
        @pl.when(far > 0)
        def _():
            ring_step(gu, far)

        @pl.loop(jnp.maximum(2 * far - 1, 0), 2 * far + 1)
        def _(turn):
            forward(block_at(turn))
            backward(block_at(turn))

        @pl.when(far > 0)
        def _():
            @pl.loop(jnp.maximum(2 * far - 3, 0), 2 * far - 1)
            def _(turn):
                finish_b(block_at(turn))

    ring_last(gu)
    final = wrap(me + half, n_local)
    forward(final)

    @pl.loop(0, hidden // part)
    def _(index):
        at = cols(index, part)
        gate = pre[:, at]
        up = pre[:, pl.ds(pl.multiple_of(hidden + index * part, part), part)]
        hid[:, at] = (gate / (1.0 + jnp.exp(-gate)) * up).astype(jnp.bfloat16)

    @pl.loop(0, n_local)
    def _(block):
        xs_a[:, cols(block)] = jnp.dot(
            hid[...], dn_v[block], preferred_element_type=jnp.float32
        ).astype(jnp.bfloat16)
        give_back(xs_a, back_a, ret_a_send, ret_a_recv, block)

    backward(final)

    @pl.loop(0, n_local)
    def _(block):
        finish_a(block)

    @pl.loop(2 * half - 3, 2 * half)
    def _(turn):
        finish_b(block_at(turn))

    ring_drain(dn)
    ring_drain(gu)

    @pl.loop(0, n_local)
    def _(block):
        all_of(xs_a, ret_a_send.at[block], cols(block)).wait()
        all_of(xs_b, ret_b_send.at[block], cols(block)).wait()

    for slot, (source, target) in enumerate(((res_a, out_a), (res_b, out_b))):
        pltpu.make_async_copy(source, source, relay_send.at[slot]).wait()
        pltpu.make_async_copy(target, target, relay_recv.at[slot]).wait()


def body(
    act_fwd, routes_fwd, weight_fwd, grad_bwd, routes_bwd, weight_bwd, saved_bwd, w_gate_up, w_down
):
    n_node, n_local = lax.axis_size("node"), lax.axis_size("local")
    tokens, features = act_fwd.shape[1:]
    hidden, column = w_down.shape[2:]
    total = n_node * ROWS
    bf16, f32 = jnp.bfloat16, jnp.float32
    anywhere = pl.BlockSpec(memory_space=pl.ANY)
    small = pl.BlockSpec(memory_space=pltpu.VMEM)
    dma = pltpu.SemaphoreType.DMA
    out = jax.ShapeDtypeStruct((tokens, features), bf16)
    next_input, prev_grad = pl.pallas_call(
        kernel,
        out_shape=(out, out),
        in_specs=[anywhere, small, small, anywhere, small, small, anywhere, anywhere, anywhere],
        out_specs=(anywhere, anywhere),
        scratch_shapes=[
            pltpu.VMEM((tokens, features), bf16),
            pltpu.VMEM((tokens, features), bf16),
            pltpu.VMEM((tokens, 2 * hidden), bf16),
            pltpu.VMEM((n_local, column, 2 * hidden), bf16),
            pltpu.VMEM((n_local, hidden, column), bf16),
            pltpu.VMEM((total, features), bf16),
            pltpu.VMEM((total, features), bf16),
            pltpu.VMEM((total, features), bf16),
            pltpu.VMEM((total, features), bf16),
            pltpu.VMEM((total, 2 * hidden), bf16),
            pltpu.VMEM((total, 2 * hidden), bf16),
            pltpu.VMEM((total, features), bf16),
            pltpu.VMEM((total, features), bf16),
            pltpu.VMEM((tokens, features), bf16),
            pltpu.VMEM((tokens, features), bf16),
            pltpu.VMEM((total, 2 * hidden), f32),
            pltpu.VMEM((total, hidden), f32),
            pltpu.VMEM((total, 2 * hidden), bf16),
            pltpu.VMEM((total, hidden), bf16),
            pltpu.VMEM((tokens, total), bf16),
            pltpu.VMEM((tokens, total), bf16),
            pltpu.VMEM((tokens, column), f32),
            dma((5,)), dma((3,)), dma((3,)),
            dma((2 * n_local,)), dma((2 * n_local,)), dma((2 * n_local,)), dma((2 * n_local,)),
            dma((n_local,)), dma((n_local,)), dma((n_local,)), dma((n_local,)),
            dma((2,)), dma((2,)),
        ],
        compiler_params=pltpu.CompilerParams(
            collective_id=0, has_side_effects=True, vmem_limit_bytes=60 * 2**20
        ),
        cost_estimate=pl.CostEstimate(flops=13 * 10**9, bytes_accessed=10 * 2**20, transcendentals=2**19),
    )(
        act_fwd[0],
        routes_fwd.reshape(1, tokens),
        weight_fwd,
        grad_bwd[0],
        routes_bwd.reshape(1, tokens),
        weight_bwd,
        saved_bwd[0],
        w_gate_up[0, 0],
        w_down[0, 0],
    )
    return (next_input[None], prev_grad[None])


def solution(mesh):
    in_specs = (
        P("pp", ("node", "local"), None),
        P("pp", ("node", "local"), None),
        P("pp", ("node", "local")),
        P("pp", ("node", "local"), None),
        P("pp", ("node", "local"), None),
        P("pp", ("node", "local")),
        P("pp", ("node", "local"), None),
        P("pp", "node", "local", None),
        P("pp", "node", None, "local"),
    )
    out_specs = (P("pp", ("node", "local"), None), P("pp", ("node", "local"), None))
    return jax.shard_map(body, mesh=mesh, in_specs=in_specs, out_specs=out_specs, check_vma=False)
```

time: 384 us -> 299 us (0.78)
  Pallas kernels: 0 us -> 295 us
  waiting for transfers between devices: 275 us -> 0 us
  matrix products: 47.5 us -> 0 us
  starting transfers between devices: 30.3 us -> 0 us
  between operations: 14.3 us -> 0.65 us
  local copies, waits for them, and re-layouts: 15.9 us -> 3.35 us
    pallas_call x0 -> x1, Pallas kernels: none -> 295 us  [body(): pl.pallas_call(kernel, out_shape=(out, out), in_specs=[anywhere, small, s...]
    all_gather x2 -> x0, waiting for transfers between devices: 188 us -> none  [the longest x1 162 us: body(): w_gu = lax.all_gather(w_gate_up[0, 0], 'local', axis=0, tiled=True)]
    all_to_all x5 -> x0, waiting for transfers between devices: 61.8 us -> none  [swap(): lax.all_to_all(blocks, 'node', split_axis=0, concat_axis=0, tiled=True)]
    dot_general x23 -> x0, matrix products: 47.5 us -> none  [the longest x8 12.5 us: body(): jnp.dot(hidden, w_dn[j], preferred_element_type=jnp.float32)]
    all_to_all x5 -> x0, starting transfers between devices: 26.4 us -> none  [swap(): lax.all_to_all(blocks, 'node', split_axis=0, concat_axis=0, tiled=True)]
    ppermute x2 -> x0, waiting for transfers between devices: 23.8 us -> none  [the longest x1 19.6 us: body(): lax.ppermute(result_a[None], 'pp', [(i, (i + 1) % length) for i in range(...]
    reshape x10 -> x0, local copies, waits for them, and re-layouts: 12 us -> none  [the longest x5 6.36 us: swap(): blocks = packed.reshape(nodes, -1, packed.shape[1])]
  transfers between devices with their start and end apart: 9 -> 0, of which waited for: 8 -> 0; matrix products, arithmetic and copies ran while one was open for 12% -> 0% of each run, Pallas kernels for 0% -> 0%
where the time goes in v1:
time: 299 us
  Pallas kernels  295 us (99%)
  local copies, waits for them, and re-layouts  3.35 us (1%)
    pallas_call x1, Pallas kernels, body(): pl.pallas_call(kernel, out_shape=(out, out), in_specs=[anywhere, small, s...  295 us

profile of v1, /device:TPU:1, one launch (start us, length us, event | category | flops | bytes accessed | tf_op | source)
XLA Modules:
  0.0 299.3 jit_solution(17425606196266335622)
XLA Ops:
  0.6 295.3 %shard_map.104 = (bf16[128,4096]{1,0:T(8,128)(2,1)}, bf16[128,4096]{1,0:T(8,128)(2,1)}) custom-call(bf16[128,4096]{1,0:T(8,128)(2,1)} %bitcast.12, s32[1,128]{1,0:T(1,128)} %bitcast.16, f32[1,128]{1,0:T(1,128)} %weight_a.1, bf16[128,4096]{1,0:T(8,128)(2,1)} %bitcast.13, s32[1,128]{1,0:T(1,128)} %bitcast.17, f32[1,128]{1,0:T(1,128)} %weight_b.1, ...), custom_call_target="tpu_custom_call" | custom-call | flops 12999999488 | bytes 10485760 | tf_op jit(solution)/shard_map/pallas_call | solution.py:346
  296.0 0.0 copy-start
  296.0 2.4 copy.13
  298.3 0.0 copy-done
  298.3 1.0 copy.14
Async XLA Ops:
  296.0 2.4 copy-start

commit v2 on v0

v2 whole, which is shorter than its diff:
```python
import functools

import jax
import jax.numpy as jnp
from jax import lax
from jax.experimental import pallas as pl
from jax.experimental.pallas import tpu as pltpu
from jax.sharding import PartitionSpec as P

MESH = pl.DeviceIdType.MESH
NT = (((1,), (1,)), ((), ()))
QUARTERS = 4
PIECES = 4
OFFSETS = (0, 1, -1, 2, -2, 3, -3, 4)


def kernel(
    capacity, act, route_a, weight_a, grad, route_b, weight_b, saved, w_gu, w_dn,
    out_a, out_b,
    act_v, grad_v, saved_v, gu_1, dn_1, gu_v, dn_v, xs_a, xr_a, xq_a, xs_b, xr_b, xq_b, ss, sr, sq,
    back_a, back_b, res_a, res_b, pre, dh, dgu, hid, put, pick_a, pick_b, scale_a, sort, unsort,
    load_sem, disp_send, disp_recv,
    dn_send_1, dn_recv_1, dn_send_2, dn_recv_2, dn_send_3, dn_recv_3, dn_recv_s,
    gu_send_1, gu_recv_1, gu_send_2, gu_recv_2, gu_send_3, gu_recv_3, gu_recv_s,
    ret_a_send, ret_a_recv, ret_b_send, ret_b_recv, relay_send, relay_recv,
):
    n_pp, n_node, n_local = lax.axis_size("pp"), lax.axis_size("node"), lax.axis_size("local")
    pp, node, me = lax.axis_index("pp"), lax.axis_index("node"), lax.axis_index("local")
    tokens, features = act.shape
    hidden, column = w_dn.shape
    slots = QUARTERS * capacity
    total = n_local * slots
    each = n_local * capacity
    width = features // QUARTERS
    piece = width // PIECES

    def wrap(index, size):
        return lax.rem(index + size, size)

    right, left = wrap(node + 2, n_node), wrap(node - 2, n_node)
    sibling = node + 1 - 2 * lax.rem(node, 2)
    ahead, behind = wrap(pp + 1, n_pp), wrap(pp - 1, n_pp)
    peers = [wrap(node + k, n_node) for k in range(1, n_node)]
    planes = [wrap(me + k, n_local) for k in range(1, n_local)]

    def rows_at(index, size):
        return pl.ds(pl.multiple_of(index * size, size), size)

    def send(source, target, send_sem, recv_sem, **to):
        pltpu.make_async_remote_copy(
            src_ref=source, dst_ref=target, send_sem=send_sem, recv_sem=recv_sem,
            device_id=to, device_id_type=MESH,
        ).start()

    def wait(ref, sem):
        pltpu.make_async_copy(ref, ref, sem).wait()

    barrier = pltpu.get_barrier_semaphore()
    for peer in peers:
        pl.semaphore_signal(barrier, inc=1, device_id={"node": peer}, device_id_type=MESH)
    for plane in planes:
        pl.semaphore_signal(barrier, inc=1, device_id={"local": plane}, device_id_type=MESH)
    for neighbour in (behind, ahead):
        pl.semaphore_signal(barrier, inc=1, device_id={"pp": neighbour}, device_id_type=MESH)

    def load(source, target, slot):
        wide = source.shape[1] // QUARTERS
        for q in range(QUARTERS):
            pltpu.make_async_copy(
                source.at[:, pl.ds(q * wide, wide)], target.at[pl.ds(q * tokens, tokens), :],
                load_sem.at[slot],
            ).start()

    load(grad, grad_v, 0)
    load(saved, saved_v, 1)
    load(act, act_v, 2)

    dn = (w_dn, dn_1, dn_v, dn_send_1, dn_recv_1, dn_send_2, dn_recv_2, dn_send_3, dn_recv_3, dn_recv_s)
    gu = (w_gu, gu_1, gu_v, gu_send_1, gu_recv_1, gu_send_2, gu_recv_2, gu_send_3, gu_recv_3, gu_recv_s)

    def step_1_own(array):
        shard, first, _, _, recv_1, *_ = array
        pltpu.make_async_copy(
            shard.at[rows_at(node, first.shape[1]), :], first.at[node], recv_1.at[node]
        ).start()

    def step_1(array):
        shard, first, _, send_1, recv_1, *_ = array
        for peer in peers:
            send(shard.at[rows_at(peer, first.shape[1]), :], first.at[node], send_1.at[0], recv_1.at[node], node=peer)

    def step_2(array):
        _, first, full, _, recv_1, send_2, recv_2, *_ = array
        size = first.shape[1]
        for k in range(n_node):
            expert = wrap(node + k, n_node)
            wait(first.at[expert], recv_1.at[expert])
            target = full.at[me, rows_at(node, size), :]

            @pl.when(expert == me)
            def _():
                pltpu.make_async_copy(first.at[expert], target, recv_2.at[me]).start()

            @pl.when(expert != me)
            def _():
                send(first.at[expert], target, send_2.at[0], recv_2.at[me], local=expert)

    def region(array, block, owner):
        size = array[1].shape[1]
        return array[2].at[block, rows_at(owner, size), :]

    def own_part(array, unit):
        send_3, recv_3, recv_s = array[-3:]
        block = wrap(me + OFFSETS[unit], n_local)
        part = region(array, block, node)
        wait(part, array[6].at[block])
        send(part, part, send_3.at[0], recv_3.at[0, block], node=right)
        send(part, part, send_3.at[1], recv_3.at[1, block], node=left)
        send(part, part, send_3.at[3], recv_s.at[block], node=sibling)

    def next_parts(array, unit):
        send_3, recv_3, recv_s = array[-3:]
        block = wrap(me + OFFSETS[unit], n_local)
        for way, owner in ((0, left), (1, right)):
            part = region(array, block, owner)
            wait(part, recv_3.at[way, block])
            if unit % 2 == way:
                send(part, part, send_3.at[2], recv_3.at[2, block], node=right if way == 0 else left)
            send(part, part, send_3.at[4 + way], recv_s.at[block], node=sibling)

    def last_part(array, unit):
        send_3, recv_3, recv_s = array[-3:]
        block = wrap(me + OFFSETS[unit], n_local)
        part = region(array, block, wrap(node + 4, n_node))
        wait(part, recv_3.at[2, block])
        send(part, part, send_3.at[6], recv_s.at[block], node=sibling)

    def whole(array, block):
        half = array[2].shape[1] // 2
        wait(array[2].at[block, pl.ds(0, half), :], array[-1].at[block])

    def drain(array):
        _, first, full, send_1, _, send_2, _, send_3, *_ = array
        size = first.shape[1]
        wait(first.at[pl.ds(0, n_node - 1)], send_1.at[0])
        wait(full.at[pl.ds(0, n_local - 1), pl.ds(0, size), :], send_2.at[0])
        for kind in range(7):
            wait(full.at[:, pl.ds(0, size), :], send_3.at[kind])

    step_1_own(dn)
    step_1_own(gu)
    pl.semaphore_wait(barrier, n_node - 1 + n_local - 1 + 2)
    step_1(dn)
    step_1(gu)

    def places(route_ref, pick):
        route = jnp.broadcast_to(route_ref[...].astype(jnp.float32), (tokens, tokens))
        turned = jnp.transpose(route)
        first = lax.broadcasted_iota(jnp.int32, (tokens, tokens), 0)
        second = lax.broadcasted_iota(jnp.int32, (tokens, tokens), 1)
        same = route == turned
        slot_row = jnp.sum(jnp.where(same & (first < second), 1.0, 0.0), axis=0, keepdims=True)
        slot_col = jnp.sum(jnp.where(same & (second < first), 1.0, 0.0), axis=1, keepdims=True)
        row = route[0:1, :] * float(slots) + slot_row
        col = turned[:, 0:1] * float(slots) + slot_col
        down = lax.broadcasted_iota(jnp.int32, (total, tokens), 0).astype(jnp.float32)
        along = lax.broadcasted_iota(jnp.int32, (tokens, total), 1).astype(jnp.float32)
        for q in range(QUARTERS):
            shift = float(q * capacity)
            put[:, q * tokens : (q + 1) * tokens] = jnp.where(down == row + shift, 1.0, 0.0).astype(jnp.bfloat16)
            pick[q * tokens : (q + 1) * tokens, :] = jnp.where(along == col + shift, 1.0, 0.0).astype(jnp.bfloat16)

    def spread(weight_ref, wide):
        turned = jnp.transpose(jnp.broadcast_to(weight_ref[...], (tokens, tokens)))
        return jnp.concatenate([turned] * (wide // tokens), axis=1)

    def multiply(left_ref, source, target, wide):
        @pl.loop(0, source.shape[1] // wide)
        def _(index):
            at = rows_at(index, wide)
            target[:, at] = jnp.dot(
                left_ref[...], source[:, at], preferred_element_type=jnp.float32
            ).astype(jnp.bfloat16)

    def dispatch(source, target, slot):
        for plane in planes:
            send(
                source.at[rows_at(plane, slots), :], target.at[rows_at(me, slots), :],
                disp_send.at[slot], disp_recv.at[slot], local=plane,
            )
        target[rows_at(me, slots), :] = source[rows_at(me, slots), :]

    def others(ref, sem, at=slice(None)):
        wait(ref.at[pl.ds(0, total - slots), at], sem)

    places(route_b, pick_b)
    scale_b = spread(weight_b, piece)
    wait(grad_v, load_sem.at[0])
    for q in range(QUARTERS):
        for p in range(PIECES):
            at = (slice(q * tokens, (q + 1) * tokens), slice(p * piece, (p + 1) * piece))
            res_b[at] = (scale_b * grad_v[at].astype(jnp.float32)).astype(jnp.bfloat16)
    multiply(put, res_b, xs_b, 512)
    dispatch(xs_b, xr_b, 0)
    wait(saved_v, load_sem.at[1])
    multiply(put, saved_v, ss, 512)
    dispatch(ss, sr, 1)
    step_2(dn)
    places(route_a, pick_a)
    scale_a[...] = spread(weight_a, piece)
    wait(act_v, load_sem.at[2])
    multiply(put, act_v, xs_a, 512)
    step_2(gu)
    dispatch(xs_a, xr_a, 2)

    def home(index):
        quarter = sum(jnp.where(index >= float(each * j), 1.0, 0.0) for j in range(1, QUARTERS))
        rest = index - quarter * float(each)
        source = sum(jnp.where(rest >= float(capacity * j), 1.0, 0.0) for j in range(1, n_local))
        return source * float(slots) + quarter * float(capacity) + rest - source * float(capacity)

    down = lax.broadcasted_iota(jnp.int32, (total, 128), 0).astype(jnp.float32)
    along = lax.broadcasted_iota(jnp.int32, (8, total), 1).astype(jnp.float32)
    to_col, to_row = home(down)[:, 0:1], home(along)[0:1, :]
    for start in range(0, total, 128):
        across = lax.broadcasted_iota(jnp.int32, (total, 128), 1).astype(jnp.float32) + float(start)
        sort[:, start : start + 128] = jnp.where(across == to_col, 1.0, 0.0).astype(jnp.bfloat16)
        unsort[:, start : start + 128] = jnp.where(down == to_row[:, start : start + 128], 1.0, 0.0).astype(jnp.bfloat16)

    def of_block(block):
        per = width // column
        quarter = lax.div(block, per)
        return rows_at(quarter, each), rows_at(block - quarter * per, column)

    def hidden_grad():
        others(xr_b, disp_recv.at[0])
        multiply(sort, xr_b, xq_b, 512)
        others(sr, disp_recv.at[1])
        multiply(sort, sr, sq, 512)
        dh[...] = jnp.zeros_like(dh)
        for unit in range(n_local):
            whole(dn, wrap(me + OFFSETS[unit], n_local))

        @pl.loop(0, n_local)
        def _(block):
            dh[...] += lax.dot_general(
                xq_b[of_block(block)], dn_v[block], NT, preferred_element_type=jnp.float32
            )

        wide = 2 * hidden // QUARTERS
        for q in range(QUARTERS // 2):
            gate = sq[q * each : (q + 1) * each, :].astype(jnp.float32)
            up = sq[(q + 2) * each : (q + 3) * each, :].astype(jnp.float32)
            grad_h = dh[:, q * wide : (q + 1) * wide]
            sigmoid = 1.0 / (1.0 + jnp.exp(-gate))
            dgu[:, q * wide : (q + 1) * wide] = (
                grad_h * up * sigmoid * (1.0 + gate * (1.0 - sigmoid))
            ).astype(jnp.bfloat16)
            dgu[:, hidden + q * wide : hidden + (q + 1) * wide] = (grad_h * gate * sigmoid).astype(jnp.bfloat16)

    def backward(unit):
        block = wrap(me + OFFSETS[unit], n_local)
        whole(gu, block)
        xq_b[of_block(block)] = lax.dot_general(
            dgu[...], gu_v[block], NT, preferred_element_type=jnp.float32
        ).astype(jnp.bfloat16)

    units = [(array, unit) for array in (dn, gu) for unit in range(n_local)]
    for turn in range(len(units) + 2):
        if turn < len(units):
            own_part(*units[turn])
        if 1 <= turn <= len(units):
            next_parts(*units[turn - 1])
        if turn >= 2:
            last_part(*units[turn - 2])
        if turn == n_local + 2:
            hidden_grad()
        if turn >= n_local + 3:
            backward(turn - n_local - 3)
    backward(n_local - 1)

    def at_piece(p):
        return slice(p * piece, (p + 1) * piece)

    def give_back(sorted_rows, source, target, send_sem, recv_sem, p):
        source[:, at_piece(p)] = jnp.dot(
            unsort[...], sorted_rows[:, at_piece(p)], preferred_element_type=jnp.float32
        ).astype(jnp.bfloat16)
        for plane in planes:
            send(
                source.at[rows_at(plane, slots), at_piece(p)], target.at[rows_at(me, slots), at_piece(p)],
                send_sem.at[p], recv_sem.at[p], local=plane,
            )
        target[rows_at(me, slots), at_piece(p)] = source[rows_at(me, slots), at_piece(p)]

    def relay(source, target, slot, to, p):
        for q in range(QUARTERS):
            send(
                source.at[pl.ds(q * tokens, tokens), at_piece(p)],
                target.at[:, pl.ds(q * width + p * piece, piece)],
                relay_send.at[slot], relay_recv.at[slot], pp=to,
            )

    def finish_b(p):
        others(back_b, ret_b_recv.at[p], at_piece(p))
        moe = jnp.dot(pick_b[...], back_b[:, at_piece(p)], preferred_element_type=jnp.float32)
        res_b[:, at_piece(p)] = (grad_v[:, at_piece(p)].astype(jnp.float32) + moe).astype(jnp.bfloat16)
        relay(res_b, out_b, 1, behind, p)

    def finish_a(p):
        others(back_a, ret_a_recv.at[p], at_piece(p))
        moe = jnp.dot(pick_a[...], back_a[:, at_piece(p)], preferred_element_type=jnp.float32)
        for q in range(QUARTERS):
            at = (slice(q * tokens, (q + 1) * tokens), at_piece(p))
            res_a[at] = (
                act_v[at].astype(jnp.float32) + scale_a[...] * moe[q * tokens : (q + 1) * tokens, :]
            ).astype(jnp.bfloat16)
        relay(res_a, out_a, 0, ahead, p)

    others(xs_b, disp_send.at[0])
    for p in range(PIECES):
        give_back(xq_b, xs_b, back_b, ret_b_send, ret_b_recv, p)

    others(xr_a, disp_recv.at[2])
    multiply(sort, xr_a, xq_a, 512)
    pre[...] = jnp.zeros_like(pre)

    @pl.loop(0, n_local)
    def _(block):
        x = xq_a[of_block(block)]

        @pl.loop(0, 2 * hidden // 512)
        def _(index):
            at = rows_at(index, 512)
            pre[:, at] += jnp.dot(x, gu_v[block, :, at], preferred_element_type=jnp.float32)

    gate = pre[:, :hidden]
    hid[...] = (gate / (1.0 + jnp.exp(-gate)) * pre[:, hidden:]).astype(jnp.bfloat16)
    others(xs_a, disp_send.at[2])
    for p in range(PIECES):
        for q in range(QUARTERS):
            begin = q * width + p * piece
            block, inner = begin // column, begin % column
            xq_a[q * each : (q + 1) * each, at_piece(p)] = jnp.dot(
                hid[...], dn_v[block, :, inner : inner + piece], preferred_element_type=jnp.float32
            ).astype(jnp.bfloat16)
        give_back(xq_a, xs_a, back_a, ret_a_send, ret_a_recv, p)
    for p in range(PIECES):
        finish_b(p)
    for p in range(PIECES):
        finish_a(p)

    drain(dn)
    drain(gu)
    others(ss, disp_send.at[1])
    for p in range(PIECES):
        others(xs_a, ret_a_send.at[p], at_piece(p))
        others(xs_b, ret_b_send.at[p], at_piece(p))
    for slot, (source, target) in enumerate(((res_a, out_a), (res_b, out_b))):
        wait(source, relay_send.at[slot])
        wait(target, relay_recv.at[slot])


def body(
    act_fwd, routes_fwd, weight_fwd, grad_bwd, routes_bwd, weight_bwd, saved_bwd, w_gate_up, w_down
):
    n_node, n_local = lax.axis_size("node"), lax.axis_size("local")
    tokens, features = act_fwd.shape[1:]
    hidden, column = w_down.shape[2:]
    capacity = 5 * tokens // (4 * n_node)
    total = n_local * QUARTERS * capacity
    each = n_local * capacity
    width = features // QUARTERS
    bf16, f32 = jnp.bfloat16, jnp.float32
    anywhere = pl.BlockSpec(memory_space=pl.ANY)
    small = pl.BlockSpec(memory_space=pltpu.VMEM)

    def dma(*shape):
        return pltpu.SemaphoreType.DMA(shape)

    stacked = pltpu.VMEM((QUARTERS * tokens, width), bf16)
    packed = pltpu.VMEM((total, width), bf16)
    packed_saved = pltpu.VMEM((total, 2 * hidden // QUARTERS), bf16)
    of_weights = [dma(1), dma(n_node), dma(1), dma(n_local), dma(7), dma(3, n_local), dma(n_local)]
    out = jax.ShapeDtypeStruct((tokens, features), bf16)
    next_input, prev_grad = pl.pallas_call(
        functools.partial(kernel, capacity),
        out_shape=(out, out),
        in_specs=[anywhere, small, small, anywhere, small, small, anywhere, anywhere, anywhere],
        out_specs=(anywhere, anywhere),
        scratch_shapes=[
            stacked, stacked,
            pltpu.VMEM((QUARTERS * tokens, 2 * hidden // QUARTERS), bf16),
            pltpu.VMEM((n_node, column // n_node, 2 * hidden), bf16),
            pltpu.VMEM((n_node, hidden // n_node, column), bf16),
            pltpu.VMEM((n_local, column, 2 * hidden), bf16),
            pltpu.VMEM((n_local, hidden, column), bf16),
            packed, packed, packed, packed, packed, packed,
            packed_saved, packed_saved, packed_saved,
            packed, packed, stacked, stacked,
            pltpu.VMEM((each, 2 * hidden), f32),
            pltpu.VMEM((each, hidden), f32),
            pltpu.VMEM((each, 2 * hidden), bf16),
            pltpu.VMEM((each, hidden), bf16),
            pltpu.VMEM((total, QUARTERS * tokens), bf16),
            pltpu.VMEM((QUARTERS * tokens, total), bf16),
            pltpu.VMEM((QUARTERS * tokens, total), bf16),
            pltpu.VMEM((tokens, width // PIECES), f32),
            pltpu.VMEM((total, total), bf16),
            pltpu.VMEM((total, total), bf16),
            dma(3), dma(3), dma(3),
            *of_weights, *of_weights,
            dma(PIECES), dma(PIECES), dma(PIECES), dma(PIECES), dma(2), dma(2),
        ],
        compiler_params=pltpu.CompilerParams(
            collective_id=0, has_side_effects=True, vmem_limit_bytes=61 * 2**20
        ),
        cost_estimate=pl.CostEstimate(flops=13 * 10**9, bytes_accessed=10 * 2**20, transcendentals=2**19),
    )(
        act_fwd[0],
        routes_fwd.reshape(1, tokens),
        weight_fwd,
        grad_bwd[0],
        routes_bwd.reshape(1, tokens),
        weight_bwd,
        saved_bwd[0],
        w_gate_up[0, 0],
        w_down[0, 0],
    )
    return (next_input[None], prev_grad[None])


def solution(mesh):
    in_specs = (
        P("pp", ("node", "local"), None),
        P("pp", ("node", "local"), None),
        P("pp", ("node", "local")),
        P("pp", ("node", "local"), None),
        P("pp", ("node", "local"), None),
        P("pp", ("node", "local")),
        P("pp", ("node", "local"), None),
        P("pp", "node", "local", None),
        P("pp", "node", None, "local"),
    )
    out_specs = (P("pp", ("node", "local"), None), P("pp", ("node", "local"), None))
    return jax.shard_map(body, mesh=mesh, in_specs=in_specs, out_specs=out_specs, check_vma=False)
```

time: 384 us -> 268 us (0.70)
  waiting for transfers between devices: 275 us -> 0 us
  Pallas kernels: 0 us -> 264 us
  matrix products: 47.5 us -> 0 us
  starting transfers between devices: 30.3 us -> 0 us
  between operations: 14.3 us -> 0.65 us
  local copies, waits for them, and re-layouts: 15.9 us -> 3.35 us
    pallas_call x0 -> x1, Pallas kernels: none -> 264 us  [body(): pl.pallas_call(functools.partial(kernel, capacity), out_shape=(out, out),...]
    all_gather x2 -> x0, waiting for transfers between devices: 188 us -> none  [the longest x1 162 us: body(): w_gu = lax.all_gather(w_gate_up[0, 0], 'local', axis=0, tiled=True)]
    all_to_all x5 -> x0, waiting for transfers between devices: 61.8 us -> none  [swap(): lax.all_to_all(blocks, 'node', split_axis=0, concat_axis=0, tiled=True)]
    dot_general x23 -> x0, matrix products: 47.5 us -> none  [the longest x8 12.5 us: body(): jnp.dot(hidden, w_dn[j], preferred_element_type=jnp.float32)]
    all_to_all x5 -> x0, starting transfers between devices: 26.4 us -> none  [swap(): lax.all_to_all(blocks, 'node', split_axis=0, concat_axis=0, tiled=True)]
    ppermute x2 -> x0, waiting for transfers between devices: 23.8 us -> none  [the longest x1 19.6 us: body(): lax.ppermute(result_a[None], 'pp', [(i, (i + 1) % length) for i in range(...]
    reshape x10 -> x0, local copies, waits for them, and re-layouts: 12 us -> none  [the longest x5 6.36 us: swap(): blocks = packed.reshape(nodes, -1, packed.shape[1])]
  transfers between devices with their start and end apart: 9 -> 0, of which waited for: 8 -> 0; matrix products, arithmetic and copies ran while one was open for 12% -> 0% of each run, Pallas kernels for 0% -> 0%
where the time goes in v2:
time: 268 us
  Pallas kernels  264 us (99%)
  local copies, waits for them, and re-layouts  3.35 us (1%)
    pallas_call x1, Pallas kernels, body(): pl.pallas_call(functools.partial(kernel, capacity), out_shape=(out, out),...  264 us

profile of v2, /device:TPU:1, one launch (start us, length us, event | category | flops | bytes accessed | tf_op | source)
XLA Modules:
  0.0 267.8 jit_solution(16408037528958085365)
XLA Ops:
  0.6 263.8 %shard_map.104 = (bf16[128,4096]{1,0:T(8,128)(2,1)}, bf16[128,4096]{1,0:T(8,128)(2,1)}) custom-call(bf16[128,4096]{1,0:T(8,128)(2,1)} %bitcast.12, s32[1,128]{1,0:T(1,128)} %bitcast.16, f32[1,128]{1,0:T(1,128)} %weight_a.1, bf16[128,4096]{1,0:T(8,128)(2,1)} %bitcast.13, s32[1,128]{1,0:T(1,128)} %bitcast.17, f32[1,128]{1,0:T(1,128)} %weight_b.1, ...), custom_call_target="tpu_custom_call" | custom-call | flops 12999999488 | bytes 10485760 | tf_op jit(solution)/shard_map/pallas_call | solution.py:386
  264.5 0.0 copy-start
  264.5 2.4 copy.13
  266.8 0.0 copy-done
  266.8 1.0 copy.14
Async XLA Ops:
  264.5 2.4 copy-start

commit v3 on v2

--- a/solution.py
+++ b/solution.py
@@ -10,15 +10,14 @@
 MESH = pl.DeviceIdType.MESH
 NT = (((1,), (1,)), ((), ()))
 QUARTERS = 4
-PIECES = 4
-OFFSETS = (0, 1, -1, 2, -2, 3, -3, 4)
+OFFSETS = (0, 2, -2, 4, 1, -1, 3, -3)
 
 
 def kernel(
     capacity, act, route_a, weight_a, grad, route_b, weight_b, saved, w_gu, w_dn,
     out_a, out_b,
     act_v, grad_v, saved_v, gu_1, dn_1, gu_v, dn_v, xs_a, xr_a, xq_a, xs_b, xr_b, xq_b, ss, sr, sq,
-    back_a, back_b, res_a, res_b, pre, dh, dgu, hid, put, pick_a, pick_b, scale_a, sort, unsort,
+    ys_a, ys_b, back_a, back_b, res_a, res_b, pre, dh, dgu, hid, put, pick_a, pick_b, scale_a, sort, unsort,
     load_sem, disp_send, disp_recv,
     dn_send_1, dn_recv_1, dn_send_2, dn_recv_2, dn_send_3, dn_recv_3, dn_recv_s,
     gu_send_1, gu_recv_1, gu_send_2, gu_recv_2, gu_send_3, gu_recv_3, gu_recv_s,
@@ -32,7 +31,6 @@
     total = n_local * slots
     each = n_local * capacity
     width = features // QUARTERS
-    piece = width // PIECES
 
     def wrap(index, size):
         return lax.rem(index + size, size)
@@ -89,20 +87,15 @@
         for peer in peers:
             send(shard.at[rows_at(peer, first.shape[1]), :], first.at[node], send_1.at[0], recv_1.at[node], node=peer)
 
-    def step_2(array):
+    def step_2(array, offsets):
         _, first, full, _, recv_1, send_2, recv_2, *_ = array
-        size = first.shape[1]
-        for k in range(n_node):
-            expert = wrap(node + k, n_node)
+        target = full.at[me, rows_at(node, first.shape[1]), :]
+        for offset in offsets:
+            expert = wrap(me - offset, n_local)
             wait(first.at[expert], recv_1.at[expert])
-            target = full.at[me, rows_at(node, size), :]
-
-            @pl.when(expert == me)
-            def _():
+            if offset == 0:
                 pltpu.make_async_copy(first.at[expert], target, recv_2.at[me]).start()
-
-            @pl.when(expert != me)
-            def _():
+            else:
                 send(first.at[expert], target, send_2.at[0], recv_2.at[me], local=expert)
 
     def region(array, block, owner):
@@ -151,7 +144,6 @@
     step_1_own(gu)
     pl.semaphore_wait(barrier, n_node - 1 + n_local - 1 + 2)
     step_1(dn)
-    step_1(gu)
 
     def places(route_ref, pick):
         route = jnp.broadcast_to(route_ref[...].astype(jnp.float32), (tokens, tokens))
@@ -182,36 +174,42 @@
                 left_ref[...], source[:, at], preferred_element_type=jnp.float32
             ).astype(jnp.bfloat16)
 
-    def dispatch(source, target, slot):
-        for plane in planes:
+    def dispatch(source, target, slot, offsets=OFFSETS[1:]):
+        for offset in offsets:
+            plane = wrap(me - offset, n_local)
             send(
                 source.at[rows_at(plane, slots), :], target.at[rows_at(me, slots), :],
                 disp_send.at[slot], disp_recv.at[slot], local=plane,
             )
+
+    def keep(source, target):
         target[rows_at(me, slots), :] = source[rows_at(me, slots), :]
 
     def others(ref, sem, at=slice(None)):
         wait(ref.at[pl.ds(0, total - slots), at], sem)
 
     places(route_b, pick_b)
-    scale_b = spread(weight_b, piece)
-    wait(grad_v, load_sem.at[0])
-    for q in range(QUARTERS):
-        for p in range(PIECES):
-            at = (slice(q * tokens, (q + 1) * tokens), slice(p * piece, (p + 1) * piece))
-            res_b[at] = (scale_b * grad_v[at].astype(jnp.float32)).astype(jnp.bfloat16)
-    multiply(put, res_b, xs_b, 512)
-    dispatch(xs_b, xr_b, 0)
     wait(saved_v, load_sem.at[1])
     multiply(put, saved_v, ss, 512)
     dispatch(ss, sr, 1)
-    step_2(dn)
+    scale_b = spread(weight_b, column)
+    scaled = xq_a.at[pl.ds(0, QUARTERS * tokens), :]
+    wait(grad_v, load_sem.at[0])
+    for q in range(QUARTERS):
+        for start in range(0, width, column):
+            at = (slice(q * tokens, (q + 1) * tokens), slice(start, start + column))
+            scaled[at] = (scale_b * grad_v[at].astype(jnp.float32)).astype(jnp.bfloat16)
+    multiply(put, scaled, xs_b, 512)
+    step_1(gu)
+    step_2(dn, OFFSETS)
+    dispatch(xs_b, xr_b, 0)
+    keep(ss, sr)
+    keep(xs_b, xr_b)
     places(route_a, pick_a)
-    scale_a[...] = spread(weight_a, piece)
+    scale_a[...] = spread(weight_a, width // QUARTERS)
     wait(act_v, load_sem.at[2])
     multiply(put, act_v, xs_a, 512)
-    step_2(gu)
-    dispatch(xs_a, xr_a, 2)
+    keep(xs_a, xr_a)
 
     def home(index):
         quarter = sum(jnp.where(index >= float(each * j), 1.0, 0.0) for j in range(1, QUARTERS))
@@ -232,21 +230,21 @@
         quarter = lax.div(block, per)
         return rows_at(quarter, each), rows_at(block - quarter * per, column)
 
-    def hidden_grad():
+    def gather_b():
+        others(sr, disp_recv.at[1])
+        multiply(sort, sr, sq, 512)
         others(xr_b, disp_recv.at[0])
         multiply(sort, xr_b, xq_b, 512)
-        others(sr, disp_recv.at[1])
-        multiply(sort, sr, sq, 512)
         dh[...] = jnp.zeros_like(dh)
-        for unit in range(n_local):
-            whole(dn, wrap(me + OFFSETS[unit], n_local))
-
-        @pl.loop(0, n_local)
-        def _(block):
-            dh[...] += lax.dot_general(
-                xq_b[of_block(block)], dn_v[block], NT, preferred_element_type=jnp.float32
-            )
-
+
+    def hidden_grad(unit):
+        block = wrap(me + OFFSETS[unit], n_local)
+        whole(dn, block)
+        dh[...] += lax.dot_general(
+            xq_b[of_block(block)], dn_v[block], NT, preferred_element_type=jnp.float32
+        )
+
+    def gate_up_grad():
         wide = 2 * hidden // QUARTERS
         for q in range(QUARTERS // 2):
             gate = sq[q * each : (q + 1) * each, :].astype(jnp.float32)
@@ -258,75 +256,33 @@
             ).astype(jnp.bfloat16)
             dgu[:, hidden + q * wide : hidden + (q + 1) * wide] = (grad_h * gate * sigmoid).astype(jnp.bfloat16)
 
+    def give_back(value, source, target, send_sem, recv_sem, index):
+        wide = source.shape[2]
+        stacked = jnp.concatenate([value[:, k * wide : (k + 1) * wide] for k in range(QUARTERS)], axis=0)
+        source[index] = jnp.dot(unsort[...], stacked, preferred_element_type=jnp.float32).astype(jnp.bfloat16)
+        for offset in OFFSETS[1:]:
+            plane = wrap(me - offset, n_local)
+            send(
+                source.at[index, rows_at(plane, slots), :], target.at[index, rows_at(me, slots), :],
+                send_sem.at[index], recv_sem.at[index], local=plane,
+            )
+        target[index, rows_at(me, slots), :] = source[index, rows_at(me, slots), :]
+
     def backward(unit):
         block = wrap(me + OFFSETS[unit], n_local)
         whole(gu, block)
-        xq_b[of_block(block)] = lax.dot_general(
+        value = lax.dot_general(
             dgu[...], gu_v[block], NT, preferred_element_type=jnp.float32
         ).astype(jnp.bfloat16)
-
-    units = [(array, unit) for array in (dn, gu) for unit in range(n_local)]
-    for turn in range(len(units) + 2):
-        if turn < len(units):
-            own_part(*units[turn])
-        if 1 <= turn <= len(units):
-            next_parts(*units[turn - 1])
-        if turn >= 2:
-            last_part(*units[turn - 2])
-        if turn == n_local + 2:
-            hidden_grad()
-        if turn >= n_local + 3:
-            backward(turn - n_local - 3)
-    backward(n_local - 1)
-
-    def at_piece(p):
-        return slice(p * piece, (p + 1) * piece)
-
-    def give_back(sorted_rows, source, target, send_sem, recv_sem, p):
-        source[:, at_piece(p)] = jnp.dot(
-            unsort[...], sorted_rows[:, at_piece(p)], preferred_element_type=jnp.float32
-        ).astype(jnp.bfloat16)
-        for plane in planes:
-            send(
-                source.at[rows_at(plane, slots), at_piece(p)], target.at[rows_at(me, slots), at_piece(p)],
-                send_sem.at[p], recv_sem.at[p], local=plane,
-            )
-        target[rows_at(me, slots), at_piece(p)] = source[rows_at(me, slots), at_piece(p)]
-
-    def relay(source, target, slot, to, p):
-        for q in range(QUARTERS):
-            send(
-                source.at[pl.ds(q * tokens, tokens), at_piece(p)],
-                target.at[:, pl.ds(q * width + p * piece, piece)],
-                relay_send.at[slot], relay_recv.at[slot], pp=to,
-            )
-
-    def finish_b(p):
-        others(back_b, ret_b_recv.at[p], at_piece(p))
-        moe = jnp.dot(pick_b[...], back_b[:, at_piece(p)], preferred_element_type=jnp.float32)
-        res_b[:, at_piece(p)] = (grad_v[:, at_piece(p)].astype(jnp.float32) + moe).astype(jnp.bfloat16)
-        relay(res_b, out_b, 1, behind, p)
-
-    def finish_a(p):
-        others(back_a, ret_a_recv.at[p], at_piece(p))
-        moe = jnp.dot(pick_a[...], back_a[:, at_piece(p)], preferred_element_type=jnp.float32)
-        for q in range(QUARTERS):
-            at = (slice(q * tokens, (q + 1) * tokens), at_piece(p))
-            res_a[at] = (
-                act_v[at].astype(jnp.float32) + scale_a[...] * moe[q * tokens : (q + 1) * tokens, :]
-            ).astype(jnp.bfloat16)
-        relay(res_a, out_a, 0, ahead, p)
-
-    others(xs_b, disp_send.at[0])
-    for p in range(PIECES):
-        give_back(xq_b, xs_b, back_b, ret_b_send, ret_b_recv, p)
-
-    others(xr_a, disp_recv.at[2])
-    multiply(sort, xr_a, xq_a, 512)
-    pre[...] = jnp.zeros_like(pre)
-
-    @pl.loop(0, n_local)
-    def _(block):
+        give_back(value, ys_b, back_b, ret_b_send, ret_b_recv, block)
+
+    def gather_a():
+        others(xr_a, disp_recv.at[2])
+        multiply(sort, xr_a, xq_a, 512)
+        pre[...] = jnp.zeros_like(pre)
+
+    def forward(unit):
+        block = wrap(me + OFFSETS[unit], n_local)
         x = xq_a[of_block(block)]
 
         @pl.loop(0, 2 * hidden // 512)
@@ -334,28 +290,109 @@
             at = rows_at(index, 512)
             pre[:, at] += jnp.dot(x, gu_v[block, :, at], preferred_element_type=jnp.float32)
 
+    def moe_rows(index, pick, back, recv_sem):
+        wait(back.at[index, pl.ds(0, total - slots), :], recv_sem.at[index])
+        return jnp.dot(pick[...], back[index], preferred_element_type=jnp.float32)
+
+    def strips(index, wide):
+        per = width // (QUARTERS * wide)
+        quarter = lax.div(index, per)
+        for k in range(QUARTERS):
+            within = (index - quarter * per) * QUARTERS * wide + k * wide
+            yield (
+                (rows_at(quarter, tokens), pl.ds(pl.multiple_of(within, wide), wide)),
+                (slice(None), rows_at(index * QUARTERS + k, wide)),
+            )
+
+    def relay(source, target, slot, to, index, wide):
+        at = rows_at(index, wide)
+        send(source.at[:, at], target.at[:, at], relay_send.at[slot], relay_recv.at[slot], pp=to)
+
+    def finish_b(index):
+        moe = moe_rows(index, pick_b, back_b, ret_b_recv)
+        wide = back_b.shape[2]
+        for k, (stack_at, at) in enumerate(strips(index, wide)):
+            res_b[at] = (
+                grad_v[stack_at].astype(jnp.float32) + moe[k * tokens : (k + 1) * tokens, :]
+            ).astype(jnp.bfloat16)
+        relay(res_b, out_b, 1, behind, index, QUARTERS * wide)
+
+    def finish_a(index):
+        moe = moe_rows(index, pick_a, back_a, ret_a_recv)
+        wide = back_a.shape[2]
+        for k, (stack_at, at) in enumerate(strips(index, wide)):
+            res_a[at] = (
+                act_v[stack_at].astype(jnp.float32) + scale_a[...] * moe[k * tokens : (k + 1) * tokens, :]
+            ).astype(jnp.bfloat16)
+        relay(res_a, out_a, 0, ahead, index, QUARTERS * wide)
+
+    def finish_b_unit(unit):
+        finish_b(wrap(me + OFFSETS[unit], n_local))
+
+    units = [(array, unit) for array in (dn, gu) for unit in range(n_local)]
+    extra = {
+        2: lambda: step_2(gu, (0, 2, -2)),
+        5: lambda: step_2(gu, (4,)),
+        6: lambda: dispatch(xs_a, xr_a, 2, (1, -1)),
+        7: lambda: step_2(gu, (1, -1)),
+        8: lambda: dispatch(xs_a, xr_a, 2, (2, -2)),
+        9: lambda: step_2(gu, (3, -3)),
+        10: lambda: dispatch(xs_a, xr_a, 2, (3, -3)),
+        11: lambda: dispatch(xs_a, xr_a, 2, (4,)),
+    }
+    for turn in range(len(units) + 4):
+        if turn in extra:
+            extra[turn]()
+        if turn < len(units):
+            own_part(*units[turn])
+        if 2 <= turn < len(units) + 2:
+            next_parts(*units[turn - 2])
+        if turn >= 4:
+            last_part(*units[turn - 4])
+        if turn == 8:
+            gather_b()
+        if 8 <= turn < 12:
+            hidden_grad(2 * turn - 16)
+            if turn < 11:
+                hidden_grad(2 * turn - 15)
+        if turn == 12:
+            hidden_grad(n_local - 1)
+            gate_up_grad()
+        if turn >= 13:
+            backward(turn - 13)
+        if turn == 17:
+            gather_a()
+        if turn >= 17:
+            forward(2 * turn - 34)
+            forward(2 * turn - 33)
+    backward(n_local - 1)
+    forward(n_local - 2)
+    forward(n_local - 1)
+
     gate = pre[:, :hidden]
     hid[...] = (gate / (1.0 + jnp.exp(-gate)) * pre[:, hidden:]).astype(jnp.bfloat16)
-    others(xs_a, disp_send.at[2])
-    for p in range(PIECES):
-        for q in range(QUARTERS):
-            begin = q * width + p * piece
-            block, inner = begin // column, begin % column
-            xq_a[q * each : (q + 1) * each, at_piece(p)] = jnp.dot(
-                hid[...], dn_v[block, :, inner : inner + piece], preferred_element_type=jnp.float32
-            ).astype(jnp.bfloat16)
-        give_back(xq_a, xs_a, back_a, ret_a_send, ret_a_recv, p)
-    for p in range(PIECES):
-        finish_b(p)
-    for p in range(PIECES):
-        finish_a(p)
+    per = width // column
+    for index in range(QUARTERS):
+        value = jnp.concatenate(
+            [
+                jnp.dot(hid[...], dn_v[index * per + k], preferred_element_type=jnp.float32).astype(jnp.bfloat16)
+                for k in range(per)
+            ],
+            axis=1,
+        )
+        give_back(value, ys_a, back_a, ret_a_send, ret_a_recv, index)
+        finish_b_unit(2 * index)
+        finish_b_unit(2 * index + 1)
+    for index in range(QUARTERS):
+        finish_a(index)
 
     drain(dn)
     drain(gu)
-    others(ss, disp_send.at[1])
-    for p in range(PIECES):
-        others(xs_a, ret_a_send.at[p], at_piece(p))
-        others(xs_b, ret_b_send.at[p], at_piece(p))
+    for slot, source in enumerate((xs_b, ss, xs_a)):
+        others(source, disp_send.at[slot])
+    for source, sem in ((ys_a, ret_a_send), (ys_b, ret_b_send)):
+        for index in range(source.shape[0]):
+            wait(source.at[index, pl.ds(0, total - slots), :], sem.at[index])
     for slot, (source, target) in enumerate(((res_a, out_a), (res_b, out_b))):
         wait(source, relay_send.at[slot])
         wait(target, relay_recv.at[slot])
@@ -397,7 +434,12 @@
             pltpu.VMEM((n_local, hidden, column), bf16),
             packed, packed, packed, packed, packed, packed,
             packed_saved, packed_saved, packed_saved,
-            packed, packed, stacked, stacked,
+            pltpu.VMEM((QUARTERS, total, width // QUARTERS), bf16),
+            pltpu.VMEM((n_local, total, column // QUARTERS), bf16),
+            pltpu.VMEM((QUARTERS, total, width // QUARTERS), bf16),
+            pltpu.VMEM((n_local, total, column // QUARTERS), bf16),
+            pltpu.VMEM((tokens, features), bf16),
+            pltpu.VMEM((tokens, features), bf16),
             pltpu.VMEM((each, 2 * hidden), f32),
             pltpu.VMEM((each, hidden), f32),
             pltpu.VMEM((each, 2 * hidden), bf16),
@@ -405,12 +447,12 @@
             pltpu.VMEM((total, QUARTERS * tokens), bf16),
             pltpu.VMEM((QUARTERS * tokens, total), bf16),
             pltpu.VMEM((QUARTERS * tokens, total), bf16),
-            pltpu.VMEM((tokens, width // PIECES), f32),
+            pltpu.VMEM((tokens, width // QUARTERS), f32),
             pltpu.VMEM((total, total), bf16),
             pltpu.VMEM((total, total), bf16),
             dma(3), dma(3), dma(3),
             *of_weights, *of_weights,
-            dma(PIECES), dma(PIECES), dma(PIECES), dma(PIECES), dma(2), dma(2),
+            dma(QUARTERS), dma(QUARTERS), dma(n_local), dma(n_local), dma(2), dma(2),
         ],
         compiler_params=pltpu.CompilerParams(
             collective_id=0, has_side_effects=True, vmem_limit_bytes=61 * 2**20

time: 268 us -> 222 us (0.83)
  Pallas kernels: 264 us -> 218 us
    pallas_call x1, Pallas kernels: 264 us -> 218 us  [body(): pl.pallas_call(functools.partial(kernel, capacity), out_shape=(out, out),...]
where the time goes in v3:
time: 222 us
  Pallas kernels  218 us (98%)
  local copies, waits for them, and re-layouts  3.35 us (2%)
    pallas_call x1, Pallas kernels, body(): pl.pallas_call(functools.partial(kernel, capacity), out_shape=(out, out),...  218 us

profile of v3, /device:TPU:1, one launch (start us, length us, event | category | flops | bytes accessed | tf_op | source)
XLA Modules:
  0.0 221.6 jit_solution(11914790870764694480)
XLA Ops:
  0.6 217.6 %shard_map.104 = (bf16[128,4096]{1,0:T(8,128)(2,1)}, bf16[128,4096]{1,0:T(8,128)(2,1)}) custom-call(bf16[128,4096]{1,0:T(8,128)(2,1)} %bitcast.12, s32[1,128]{1,0:T(1,128)} %bitcast.16, f32[1,128]{1,0:T(1,128)} %weight_a.1, bf16[128,4096]{1,0:T(8,128)(2,1)} %bitcast.13, s32[1,128]{1,0:T(1,128)} %bitcast.17, f32[1,128]{1,0:T(1,128)} %weight_b.1, ...), custom_call_target="tpu_custom_call" | custom-call | flops 12999999488 | bytes 10485760 | tf_op jit(solution)/shard_map/pallas_call | solution.py:423
  218.2 0.0 copy-start
  218.3 2.4 %copy.13 = bf16[1,128,4096]{2,1,0:T(8,128)(2,1)} copy(bf16[1,128,4096]{2,1,0:T(8,128)(2,1)} %bitcast.10) | data formatting | bytes 2097152
  220.6 0.0 copy-done
  220.6 1.0 copy.14
Async XLA Ops:
  218.2 2.4 %copy-start = (bf16[128,4096]{1,0:T(8,128)(2,1)S(1)}, bf16[128,4096]{1,0:T(8,128)(2,1)}, u32[]{:S(2)}) copy-start(bf16[128,4096]{1,0:T(8,128)(2,1)} %get-tuple-element.5) | copy-start | bytes 3145732

commit v4 on v3

--- a/solution.py
+++ b/solution.py
@@ -17,7 +17,7 @@
     capacity, act, route_a, weight_a, grad, route_b, weight_b, saved, w_gu, w_dn,
     out_a, out_b,
     act_v, grad_v, saved_v, gu_1, dn_1, gu_v, dn_v, xs_a, xr_a, xq_a, xs_b, xr_b, xq_b, ss, sr, sq,
-    ys_a, ys_b, back_a, back_b, res_a, res_b, pre, dh, dgu, hid, put, pick_a, pick_b, scale_a, sort, unsort,
+    ys_a, ys_b, back_a, back_b, res_a, res_b, pre, dh, dgu, hid, put, pick_a, pick_b, scale_a, sort, spare,
     load_sem, disp_send, disp_recv,
     dn_send_1, dn_recv_1, dn_send_2, dn_recv_2, dn_send_3, dn_recv_3, dn_recv_s,
     gu_send_1, gu_recv_1, gu_send_2, gu_recv_2, gu_send_3, gu_recv_3, gu_recv_s,
@@ -218,12 +218,10 @@
         return source * float(slots) + quarter * float(capacity) + rest - source * float(capacity)
 
     down = lax.broadcasted_iota(jnp.int32, (total, 128), 0).astype(jnp.float32)
-    along = lax.broadcasted_iota(jnp.int32, (8, total), 1).astype(jnp.float32)
-    to_col, to_row = home(down)[:, 0:1], home(along)[0:1, :]
+    to_col = home(down)[:, 0:1]
     for start in range(0, total, 128):
         across = lax.broadcasted_iota(jnp.int32, (total, 128), 1).astype(jnp.float32) + float(start)
         sort[:, start : start + 128] = jnp.where(across == to_col, 1.0, 0.0).astype(jnp.bfloat16)
-        unsort[:, start : start + 128] = jnp.where(down == to_row[:, start : start + 128], 1.0, 0.0).astype(jnp.bfloat16)
 
     def of_block(block):
         per = width // column
@@ -258,8 +256,13 @@
 
     def give_back(value, source, target, send_sem, recv_sem, index):
         wide = source.shape[2]
-        stacked = jnp.concatenate([value[:, k * wide : (k + 1) * wide] for k in range(QUARTERS)], axis=0)
-        source[index] = jnp.dot(unsort[...], stacked, preferred_element_type=jnp.float32).astype(jnp.bfloat16)
+        for origin in range(n_local):
+            for k in range(QUARTERS):
+                begin = origin * slots + k * capacity
+                spare[begin : begin + capacity, :wide] = value[
+                    origin * capacity : (origin + 1) * capacity, k * wide : (k + 1) * wide
+                ]
+        source[index] = spare[:, :wide].astype(jnp.bfloat16)
         for offset in OFFSETS[1:]:
             plane = wrap(me - offset, n_local)
             send(
@@ -270,10 +273,7 @@
 
     def backward(unit):
         block = wrap(me + OFFSETS[unit], n_local)
-        whole(gu, block)
-        value = lax.dot_general(
-            dgu[...], gu_v[block], NT, preferred_element_type=jnp.float32
-        ).astype(jnp.bfloat16)
+        value = lax.dot_general(dgu[...], gu_v[block], NT, preferred_element_type=jnp.float32)
         give_back(value, ys_b, back_b, ret_b_send, ret_b_recv, block)
 
     def gather_a():
@@ -290,44 +290,39 @@
             at = rows_at(index, 512)
             pre[:, at] += jnp.dot(x, gu_v[block, :, at], preferred_element_type=jnp.float32)
 
-    def moe_rows(index, pick, back, recv_sem):
-        wait(back.at[index, pl.ds(0, total - slots), :], recv_sem.at[index])
-        return jnp.dot(pick[...], back[index], preferred_element_type=jnp.float32)
-
-    def strips(index, wide):
-        per = width // (QUARTERS * wide)
-        quarter = lax.div(index, per)
+    def relay(source, target, slot, to, index):
+        at = rows_at(index, width)
+        send(source.at[:, at], target.at[:, at], relay_send.at[slot], relay_recv.at[slot], pp=to)
+
+    def strip(index, block, k, wide):
+        within = (block * QUARTERS + k) * wide
+        return (
+            (slice(index * tokens, (index + 1) * tokens), slice(within, within + wide)),
+            (slice(None), slice(index * width + within, index * width + within + wide)),
+        )
+
+    def finish_b(index):
+        per, wide = width // column, back_b.shape[2]
+        for block in range(per):
+            wait(back_b.at[index * per + block, pl.ds(0, total - slots), :], ret_b_recv.at[index * per + block])
+        both = jnp.concatenate([back_b[index * per + block] for block in range(per)], axis=1)
+        moe = jnp.dot(pick_b[...], both, preferred_element_type=jnp.float32)
+        for block in range(per):
+            for k in range(QUARTERS):
+                stack_at, at = strip(index, block, k, wide)
+                part = moe[k * tokens : (k + 1) * tokens, block * wide : (block + 1) * wide]
+                res_b[at] = (grad_v[stack_at].astype(jnp.float32) + part).astype(jnp.bfloat16)
+        relay(res_b, out_b, 1, behind, index)
+
+    def finish_a(index):
+        wide = back_a.shape[2]
+        wait(back_a.at[index, pl.ds(0, total - slots), :], ret_a_recv.at[index])
+        moe = jnp.dot(pick_a[...], back_a[index], preferred_element_type=jnp.float32)
         for k in range(QUARTERS):
-            within = (index - quarter * per) * QUARTERS * wide + k * wide
-            yield (
-                (rows_at(quarter, tokens), pl.ds(pl.multiple_of(within, wide), wide)),
-                (slice(None), rows_at(index * QUARTERS + k, wide)),
-            )
-
-    def relay(source, target, slot, to, index, wide):
-        at = rows_at(index, wide)
-        send(source.at[:, at], target.at[:, at], relay_send.at[slot], relay_recv.at[slot], pp=to)
-
-    def finish_b(index):
-        moe = moe_rows(index, pick_b, back_b, ret_b_recv)
-        wide = back_b.shape[2]
-        for k, (stack_at, at) in enumerate(strips(index, wide)):
-            res_b[at] = (
-                grad_v[stack_at].astype(jnp.float32) + moe[k * tokens : (k + 1) * tokens, :]
-            ).astype(jnp.bfloat16)
-        relay(res_b, out_b, 1, behind, index, QUARTERS * wide)
-
-    def finish_a(index):
-        moe = moe_rows(index, pick_a, back_a, ret_a_recv)
-        wide = back_a.shape[2]
-        for k, (stack_at, at) in enumerate(strips(index, wide)):
-            res_a[at] = (
-                act_v[stack_at].astype(jnp.float32) + scale_a[...] * moe[k * tokens : (k + 1) * tokens, :]
-            ).astype(jnp.bfloat16)
-        relay(res_a, out_a, 0, ahead, index, QUARTERS * wide)
-
-    def finish_b_unit(unit):
-        finish_b(wrap(me + OFFSETS[unit], n_local))
+            stack_at, at = strip(index, 0, k, wide)
+            part = moe[k * tokens : (k + 1) * tokens, :]
+            res_a[at] = (act_v[stack_at].astype(jnp.float32) + scale_a[...] * part).astype(jnp.bfloat16)
+        relay(res_a, out_a, 0, ahead, index)
 
     units = [(array, unit) for array in (dn, gu) for unit in range(n_local)]
     extra = {
@@ -359,14 +354,15 @@
             hidden_grad(n_local - 1)
             gate_up_grad()
         if turn >= 13:
+            whole(gu, wrap(me + OFFSETS[turn - 13], n_local))
             backward(turn - 13)
         if turn == 17:
             gather_a()
         if turn >= 17:
             forward(2 * turn - 34)
             forward(2 * turn - 33)
-    backward(n_local - 1)
     forward(n_local - 2)
+    whole(gu, wrap(me + OFFSETS[n_local - 1], n_local))
     forward(n_local - 1)
 
     gate = pre[:, :hidden]
@@ -375,14 +371,17 @@
     for index in range(QUARTERS):
         value = jnp.concatenate(
             [
-                jnp.dot(hid[...], dn_v[index * per + k], preferred_element_type=jnp.float32).astype(jnp.bfloat16)
+                jnp.dot(hid[...], dn_v[index * per + k], preferred_element_type=jnp.float32)
                 for k in range(per)
             ],
             axis=1,
         )
         give_back(value, ys_a, back_a, ret_a_send, ret_a_recv, index)
-        finish_b_unit(2 * index)
-        finish_b_unit(2 * index + 1)
+        if index == 0:
+            backward(n_local - 1)
+        if index > 0:
+            finish_b(index - 1)
+    finish_b(QUARTERS - 1)
     for index in range(QUARTERS):
         finish_a(index)
 
@@ -449,7 +448,7 @@
             pltpu.VMEM((QUARTERS * tokens, total), bf16),
             pltpu.VMEM((tokens, width // QUARTERS), f32),
             pltpu.VMEM((total, total), bf16),
-            pltpu.VMEM((total, total), bf16),
+            pltpu.VMEM((total, width // QUARTERS), f32),
             dma(3), dma(3), dma(3),
             *of_weights, *of_weights,
             dma(QUARTERS), dma(QUARTERS), dma(n_local), dma(n_local), dma(2), dma(2),

time: 222 us -> 221 us (level)
  Pallas kernels: 218 us -> 215 us
    pallas_call x1, Pallas kernels: 218 us -> 215 us  [body(): pl.pallas_call(functools.partial(kernel, capacity), out_shape=(out, out),...]
where the time goes in v4:
time: 221 us; the launch traced here: 219 us
  Pallas kernels  215 us (97%)
  local copies, waits for them, and re-layouts  3.35 us (2%)
    pallas_call x1, Pallas kernels, body(): pl.pallas_call(functools.partial(kernel, capacity), out_shape=(out, out),...  215 us

profile of v4, /device:TPU:1, one launch (start us, length us, event | category | flops | bytes accessed | tf_op | source)
XLA Modules:
  0.0 218.8 jit_solution(10710527781494138637)
XLA Ops:
  0.6 214.8 %shard_map.104 = (bf16[128,4096]{1,0:T(8,128)(2,1)}, bf16[128,4096]{1,0:T(8,128)(2,1)}) custom-call(bf16[128,4096]{1,0:T(8,128)(2,1)} %bitcast.12, s32[1,128]{1,0:T(1,128)} %bitcast.16, f32[1,128]{1,0:T(1,128)} %weight_a.1, bf16[128,4096]{1,0:T(8,128)(2,1)} %bitcast.13, s32[1,128]{1,0:T(1,128)} %bitcast.17, f32[1,128]{1,0:T(1,128)} %weight_b.1, ...), custom_call_target="tpu_custom_call" | custom-call | flops 12999999488 | bytes 10485760 | tf_op jit(solution)/shard_map/pallas_call | solution.py:422
  215.4 0.0 copy-start
  215.4 2.4 %copy.13 = bf16[1,128,4096]{2,1,0:T(8,128)(2,1)} copy(bf16[1,128,4096]{2,1,0:T(8,128)(2,1)} %bitcast.10) | data formatting | bytes 2097152
  217.8 0.0 copy-done
  217.8 1.0 copy.14
Async XLA Ops:
  215.4 2.4 %copy-start = (bf16[128,4096]{1,0:T(8,128)(2,1)S(1)}, bf16[128,4096]{1,0:T(8,128)(2,1)}, u32[]{:S(2)}) copy-start(bf16[128,4096]{1,0:T(8,128)(2,1)} %get-tuple-element.5) | copy-start | bytes 3145732
